TPU v7x, 32 devices: a whole 2x2x4 slice. The times are simulated.
32 devices in a mesh: dp: 16 (over z, y, core), mp: 2 (over x).
Axes of the slice: x: 2, y: 2, z: 4, core: 2. Of those that a mesh axis runs over, the one named last changes fastest.
Arguments:
- inputs: bfloat16 [16, 1024, 512], P('dp', 'mp'), may hold values from -6 to 6
- lengths: int32 [16], P('dp'), may hold values from 768 to 1024, as said below
- gain_glu: float32 [512], replicated, may hold values from 0.5 to 1.5
- w_value: bfloat16 [512, 512], P(None, 'mp'), may hold values from -0.25 to 0.25
- w_gate: bfloat16 [512, 512], P(None, 'mp'), may hold values from -0.25 to 0.25
- gain_branch: float32 [512], replicated, may hold values from 0.5 to 1.5
- w_left: bfloat16 [512, 2048], P(None, 'mp'), may hold values from -0.25 to 0.25
- w_right: bfloat16 [3, 512, 256], P(None, None, 'mp'), may hold values from -0.15625 to 0.15625
- gain_mid: bfloat16 [2048], P('mp'), may hold values from 0.5 to 1.5
- w_depth: bfloat16 [9, 2048], P(None, 'mp'), may hold values from -2 to 2
- w_point: bfloat16 [2048, 256], P('mp'), may hold values from -0.125 to 0.125
- gain_attn: float32 [512], replicated, may hold values from 0.5 to 1.5
- w_qkv: bfloat16 [3, 512, 512], P(None, None, 'mp'), may hold values from -0.25 to 0.25
- w_out: bfloat16 [512, 512], P('mp'), may hold values from -4 to 4
- gain_ffn: float32 [512], replicated, may hold values from 0.5 to 1.5
- w_in: bfloat16 [512, 2048], P(None, 'mp'), may hold values from -0.25 to 0.25
- w_back: bfloat16 [2048, 512], P('mp'), may hold values from -0.125 to 0.125
- cotangent: bfloat16 [16, 1024, 512], P('dp', 'mp'), may hold values from -6 to 6
Outputs:
- outputs: bfloat16 [16, 1024, 512], P('dp', 'mp')
- grad_inputs: bfloat16 [16, 1024, 512], P('dp', 'mp')
- grad_gain_glu: float32 [512], replicated
- grad_w_value: float32 [512, 512], P(None, 'mp')
- grad_w_gate: float32 [512, 512], P(None, 'mp')
- grad_gain_branch: float32 [512], replicated
- grad_w_left: float32 [512, 2048], P(None, 'mp')
- grad_w_right: float32 [3, 512, 256], P(None, None, 'mp')
- grad_gain_mid: float32 [2048], P('mp')
- grad_w_depth: float32 [9, 2048], P(None, 'mp')
- grad_w_point: float32 [2048, 256], P('mp')
- grad_gain_attn: float32 [512], replicated
- grad_w_qkv: float32 [3, 512, 512], P(None, None, 'mp')
- grad_w_out: float32 [512, 512], P('mp')
- grad_gain_ffn: float32 [512], replicated
- grad_w_in: float32 [512, 2048], P(None, 'mp')
- grad_w_back: float32 [2048, 512], P('mp')
Inputs may be any that keep to these rules, and one draw needn't show every extreme that they name: `lengths`: in each block of 1 sequence of one index of dp, one sequence, drawn from the seed, is 768 or more long; where a block holds two or more sequences, the others are 256 or more long. The least and the most are each taken by some sequence.
All inputs are finite; a program needn't handle non-finite values.
Results may differ from a plain program's by a relative error of at most 0.029.
Values may be sent and summed in bfloat16 or wider, within the bound.
No kernel may reach another device: no remote copies, remote signals or barrier semaphores. Data moves between devices by JAX's collectives and lax.ppermute only.
A program may use at most 192 MiB of HBM per device.

v0:
```python
import math

import jax
import jax.numpy as jnp
from jax import lax
from jax.sharding import PartitionSpec as P

FF = 2048
HEAD_DIM = 64


epsilon = 1e-06
negative_big = -1e30


def matmul(left_side, right_side):
    return jnp.dot(left_side, right_side, preferred_element_type=jnp.float32)


def contract_rows(left_side, right_side):
    return lax.dot_general(
        left_side, right_side, (((0,), (0,)), ((), ())), preferred_element_type=jnp.float32
    )


def contract_cols(left_side, right_side):
    return lax.dot_general(
        left_side, right_side, (((1,), (1,)), ((), ())), preferred_element_type=jnp.float32
    )


def spread_rows(pieces):
    return lax.all_gather(pieces, "mp", axis=1, tiled=True)


def collect_rows(partial_value):
    return lax.psum_scatter(
        partial_value.astype(jnp.bfloat16), "mp", scatter_dimension=1, tiled=True
    ).astype(jnp.float32)


def channel_sums(former, latter):
    return lax.psum((jnp.sum(former, axis=-1), jnp.sum(latter, axis=-1)), "mp")


def normalize(values, gain_vec):
    centre = values - jnp.mean(values, axis=-1, keepdims=True)
    scale_inv = lax.rsqrt(jnp.mean(centre * centre, axis=-1, keepdims=True) + epsilon)
    unit_rows = centre * scale_inv
    return (unit_rows * gain_vec, unit_rows, scale_inv)


def normalize_back(grad_out, unit_rows, scale_inv, gain_vec):
    scaled = grad_out * gain_vec
    mean_one = jnp.mean(scaled, axis=-1, keepdims=True)
    mean_two = jnp.mean(scaled * unit_rows, axis=-1, keepdims=True)
    grad_in = scale_inv * (scaled - mean_one - unit_rows * mean_two)
    return (grad_in, jnp.sum(grad_out * unit_rows, axis=(0, 1)))


def silu_slope(values):
    sigmoid_part = jax.nn.sigmoid(values)
    return sigmoid_part * (1.0 + values * (1.0 - sigmoid_part))


def shifted(values, offset):
    if offset == 0:
        return values
    margin = abs(offset)
    seq_len = values.shape[1]
    filler = jnp.zeros(values.shape[:1] + (margin,) + values.shape[2:], values.dtype)
    padded = jnp.concatenate([filler, values, filler], axis=1)
    return lax.slice_in_dim(padded, margin + offset, margin + offset + seq_len, axis=1)


def place_right(right_vals, stride):
    filler = jnp.zeros(right_vals.shape + (stride - 1,), right_vals.dtype)
    joined = jnp.concatenate([right_vals[..., None], filler], axis=-1)
    return joined.reshape(right_vals.shape[:-1] + (right_vals.shape[-1] * stride,))


def attend_forward(queries, key_vecs, value_vecs, key_valid, block_rows, score_scale):
    contexts = []
    log_parts = []
    for row_start in range(0, queries.shape[0], block_rows):
        query_rows = queries[row_start : row_start + block_rows]
        scores = (
            jnp.einsum("qhd,khd->hqk", query_rows, key_vecs, preferred_element_type=jnp.float32)
            * score_scale
        )
        scores = jnp.where(key_valid[None, None, :], scores, negative_big)
        row_max = jnp.max(scores, axis=-1, keepdims=True)
        weights_exp = jnp.exp(scores - row_max)
        row_total = jnp.sum(weights_exp, axis=-1, keepdims=True)
        probability = (weights_exp / row_total).astype(jnp.bfloat16)
        contexts.append(
            jnp.einsum("hqk,khd->qhd", probability, value_vecs, preferred_element_type=jnp.float32)
        )
        log_parts.append((row_max + jnp.log(row_total))[..., 0])
    return (jnp.concatenate(contexts, axis=0), jnp.concatenate(log_parts, axis=1))


def attend_back(
    queries, key_vecs, value_vecs, key_valid, log_sums, grad_context, block_rows, score_scale
):
    grad_queries = []
    grad_keys = jnp.zeros(key_vecs.shape, jnp.float32)
    grad_values = jnp.zeros(value_vecs.shape, jnp.float32)
    for row_start in range(0, queries.shape[0], block_rows):
        query_rows = queries[row_start : row_start + block_rows]
        grad_rows = grad_context[row_start : row_start + block_rows]
        log_rows = log_sums[:, row_start : row_start + block_rows]
        scores = (
            jnp.einsum("qhd,khd->hqk", query_rows, key_vecs, preferred_element_type=jnp.float32)
            * score_scale
        )
        scores = jnp.where(key_valid[None, None, :], scores, negative_big)
        probability = jnp.exp(scores - log_rows[..., None])
        grad_prob = jnp.einsum(
            "qhd,khd->hqk", grad_rows, value_vecs, preferred_element_type=jnp.float32
        )
        row_dot = jnp.sum(probability * grad_prob, axis=-1, keepdims=True)
        grad_scores = (probability * (grad_prob - row_dot)).astype(jnp.bfloat16)
        grad_queries.append(
            jnp.einsum("hqk,khd->qhd", grad_scores, key_vecs, preferred_element_type=jnp.float32)
            * score_scale
        )
        grad_keys = (
            grad_keys
            + jnp.einsum(
                "hqk,qhd->khd", grad_scores, query_rows, preferred_element_type=jnp.float32
            )
            * score_scale
        )
        grad_values = grad_values + jnp.einsum(
            "hqk,qhd->khd",
            probability.astype(jnp.bfloat16),
            grad_rows,
            preferred_element_type=jnp.float32,
        )
    grad_query_all = jnp.concatenate(grad_queries, axis=0)
    return (grad_query_all.astype(jnp.bfloat16), grad_keys, grad_values)


def split_pass(
    inputs,
    lengths,
    gain_glu,
    w_value,
    w_gate,
    gain_branch,
    w_left,
    w_right,
    gain_mid,
    w_depth,
    w_point,
    gain_attn,
    w_qkv,
    w_out,
    gain_ffn,
    w_in,
    w_back,
    cotangent,
):
    seqs_here, local_len, model_width = inputs.shape
    group_size = lax.axis_size("mp")
    member = lax.axis_index("mp")
    seq_len = local_len * group_size
    group_rows = seqs_here * seq_len
    positions = lax.broadcasted_iota(jnp.int32, (seqs_here, seq_len), 1)
    key_valid = positions < lengths[:, None]
    valid_full = key_valid.astype(jnp.float32)
    valid_own = lax.dynamic_slice_in_dim(valid_full, member * local_len, local_len, axis=1)
    inner_cols = w_left.shape[1]
    right_cols = w_right.shape[2]
    stride = inner_cols // right_cols
    conv_taps = w_right.shape[0]
    sep_taps = w_depth.shape[0]
    sep_width = w_point.shape[1]
    head_cols = w_qkv.shape[2]
    heads_here = head_cols // HEAD_DIM
    score_scale = 1.0 / math.sqrt(HEAD_DIM)
    block_rows = min(512, seq_len)
    group_shape = (seqs_here, seq_len, model_width)
    depth_taps = w_depth.astype(jnp.float32)
    gain_mid_f = gain_mid.astype(jnp.float32)

    def branch_inner(gathered):
        flat_rows = gathered.reshape(group_rows, model_width)
        left_pre = matmul(flat_rows, w_left).reshape(seqs_here, seq_len, inner_cols)
        right_pre = jnp.zeros((group_rows, right_cols), jnp.float32)
        for tap_index in range(conv_taps):
            moved = shifted(gathered, tap_index - conv_taps // 2).reshape(group_rows, model_width)
            right_pre = right_pre + matmul(moved, w_right[tap_index])
        right_pre = right_pre.reshape(seqs_here, seq_len, right_cols)
        mid = jax.nn.silu(left_pre) + place_right(jax.nn.silu(right_pre), stride)
        return (left_pre, right_pre, mid)

    def depth_mix(depth_in):
        depth = jnp.zeros(depth_in.shape, jnp.float32)
        for tap_index in range(sep_taps):
            depth = depth + shifted(depth_in, tap_index - sep_taps // 2) * depth_taps[tap_index]
        return depth.astype(jnp.bfloat16)

    def project_qkv(gathered):
        flat_rows = gathered.reshape(group_rows, model_width)
        joined = jnp.einsum("td,kdc->ktc", flat_rows, w_qkv, preferred_element_type=jnp.float32)
        return joined.astype(jnp.bfloat16).reshape(3, seqs_here, seq_len, heads_here, HEAD_DIM)

    def forward_one(pieces):
        return attend_forward(pieces[0], pieces[1], pieces[2], pieces[3], block_rows, score_scale)

    def backward_one(pieces):
        return attend_back(
            pieces[0],
            pieces[1],
            pieces[2],
            pieces[3],
            pieces[4],
            pieces[5],
            block_rows,
            score_scale,
        )

    resid_in = inputs.astype(jnp.float32)
    normed_glu, unit_glu, inv_glu = normalize(resid_in, gain_glu)
    gathered_glu = spread_rows(normed_glu.astype(jnp.bfloat16))
    flat_glu = gathered_glu.reshape(group_rows, model_width)
    value_pre = matmul(flat_glu, w_value)
    gate_sig = jax.nn.sigmoid(matmul(flat_glu, w_gate))
    glu_local = (value_pre * gate_sig).astype(jnp.bfloat16).reshape(seqs_here, seq_len, -1)
    glu_rows = lax.all_to_all(glu_local, "mp", split_axis=1, concat_axis=2, tiled=True)
    resid_one = resid_in + glu_rows.astype(jnp.float32)
    normed_branch, unit_branch, inv_branch = normalize(resid_one, gain_branch)
    gathered_branch = spread_rows((valid_own[..., None] * normed_branch).astype(jnp.bfloat16))
    left_pre, right_pre, mid = branch_inner(gathered_branch)
    mid_sum, mid_square = channel_sums(mid, mid * mid)
    mid_mean = mid_sum / FF
    inv_mid = lax.rsqrt(mid_square / FF - mid_mean * mid_mean + epsilon)
    unit_mid = (mid - mid_mean[..., None]) * inv_mid[..., None]
    depth_in = valid_full[..., None] * unit_mid * gain_mid_f
    depth_low = depth_mix(depth_in)
    sep_part = matmul(depth_low.reshape(group_rows, inner_cols), w_point).reshape(
        seqs_here, seq_len, sep_width
    )
    sep_rows = collect_rows(sep_part)
    resid_two = resid_one + jnp.pad(sep_rows, ((0, 0), (0, 0), (0, model_width - sep_width)))
    normed_attn, unit_attn, inv_attn = normalize(resid_two, gain_attn)
    gathered_attn = spread_rows(normed_attn.astype(jnp.bfloat16))
    qkv_heads = project_qkv(gathered_attn)
    context, log_sums = lax.map(forward_one, (qkv_heads[0], qkv_heads[1], qkv_heads[2], key_valid))
    context_low = context.astype(jnp.bfloat16).reshape(group_rows, head_cols)
    attn_rows = collect_rows(matmul(context_low, w_out).reshape(group_shape))
    resid_three = resid_two + attn_rows
    normed_ffn, unit_ffn, inv_ffn = normalize(resid_three, gain_ffn)
    gathered_ffn = spread_rows(normed_ffn.astype(jnp.bfloat16))
    ffn_flat = gathered_ffn.reshape(group_rows, model_width)
    ffn_pre = matmul(ffn_flat, w_in)
    ffn_hidden = jax.nn.silu(ffn_pre).astype(jnp.bfloat16)
    final_rows = resid_three + collect_rows(matmul(ffn_hidden, w_back).reshape(group_shape))
    outputs = final_rows.astype(jnp.bfloat16)
    cot_full = spread_rows(cotangent).reshape(group_rows, model_width)
    ffn_flat = spread_rows(normed_ffn.astype(jnp.bfloat16)).reshape(group_rows, model_width)
    ffn_pre = matmul(ffn_flat, w_in)
    ffn_hidden = jax.nn.silu(ffn_pre).astype(jnp.bfloat16)
    grad_hidden = contract_cols(cot_full, w_back)
    grad_ffn_pre = (grad_hidden * silu_slope(ffn_pre)).astype(jnp.bfloat16)
    grad_w_back = contract_rows(ffn_hidden, cot_full)
    grad_w_in = contract_rows(ffn_flat, grad_ffn_pre)
    grad_normed_ffn = collect_rows(contract_cols(grad_ffn_pre, w_in).reshape(group_shape))
    grad_resid, grad_gain_ffn = normalize_back(grad_normed_ffn, unit_ffn, inv_ffn, gain_ffn)
    grad_three = cotangent.astype(jnp.float32) + grad_resid
    grad_attn = spread_rows(grad_three.astype(jnp.bfloat16)).reshape(group_rows, model_width)
    gathered_attn = spread_rows(normed_attn.astype(jnp.bfloat16))
    qkv_heads = project_qkv(gathered_attn)
    attn_flat = gathered_attn.reshape(group_rows, model_width)
    grad_w_out = contract_rows(context_low, grad_attn)
    grad_context = contract_cols(grad_attn, w_out).astype(jnp.bfloat16)
    grad_context = grad_context.reshape(seqs_here, seq_len, heads_here, HEAD_DIM)
    grad_q, grad_k, grad_v = lax.map(
        backward_one, (qkv_heads[0], qkv_heads[1], qkv_heads[2], key_valid, log_sums, grad_context)
    )
    grad_qkv = jnp.stack(
        [grad_q, grad_k.astype(jnp.bfloat16), grad_v.astype(jnp.bfloat16)]
    ).reshape(3, group_rows, head_cols)
    grad_w_qkv = jnp.einsum("td,ktc->kdc", attn_flat, grad_qkv, preferred_element_type=jnp.float32)
    grad_attn_in = jnp.einsum("ktc,kdc->td", grad_qkv, w_qkv, preferred_element_type=jnp.float32)
    grad_normed_attn = collect_rows(grad_attn_in.reshape(group_shape))
    grad_resid, grad_gain_attn = normalize_back(grad_normed_attn, unit_attn, inv_attn, gain_attn)
    grad_two = grad_three + grad_resid
    grad_sep = spread_rows(grad_two[..., :sep_width].astype(jnp.bfloat16)).reshape(
        group_rows, sep_width
    )
    gathered_branch = spread_rows((valid_own[..., None] * normed_branch).astype(jnp.bfloat16))
    left_pre, right_pre, mid = branch_inner(gathered_branch)
    unit_mid = (mid - mid_mean[..., None]) * inv_mid[..., None]
    depth_in = valid_full[..., None] * unit_mid * gain_mid_f
    depth_low = depth_mix(depth_in)
    grad_w_point = contract_rows(depth_low.reshape(group_rows, inner_cols), grad_sep)
    grad_depth = contract_cols(grad_sep, w_point).reshape(seqs_here, seq_len, inner_cols)
    grad_depth_in = jnp.zeros(grad_depth.shape, jnp.float32)
    depth_rows = []
    for tap_index in range(sep_taps):
        offset = tap_index - sep_taps // 2
        grad_depth_in = grad_depth_in + shifted(grad_depth, -offset) * depth_taps[tap_index]
        depth_rows.append(jnp.sum(shifted(depth_in, offset) * grad_depth, axis=(0, 1)))
    grad_w_depth = jnp.stack(depth_rows)
    grad_unit = grad_depth_in * valid_full[..., None]
    grad_gain_mid = jnp.sum(grad_unit * unit_mid, axis=(0, 1))
    scaled = grad_unit * gain_mid_f
    sum_one, sum_two = channel_sums(scaled, scaled * unit_mid)
    grad_mid = inv_mid[..., None] * (
        scaled - (sum_one / FF)[..., None] - unit_mid * (sum_two / FF)[..., None]
    )
    grad_left = (
        (grad_mid * silu_slope(left_pre)).astype(jnp.bfloat16).reshape(group_rows, inner_cols)
    )
    grad_right_act = grad_mid.reshape(seqs_here, seq_len, right_cols, stride)[..., 0]
    grad_right = (
        (grad_right_act * silu_slope(right_pre))
        .astype(jnp.bfloat16)
        .reshape(group_rows, right_cols)
    )
    branch_flat = gathered_branch.reshape(group_rows, model_width)
    grad_w_left = contract_rows(branch_flat, grad_left)
    grad_branch_in = contract_cols(grad_left, w_left).reshape(group_shape)
    right_rows = []
    for tap_index in range(conv_taps):
        offset = tap_index - conv_taps // 2
        moved = shifted(gathered_branch, offset).reshape(group_rows, model_width)
        right_rows.append(contract_rows(moved, grad_right))
        grad_branch_in = grad_branch_in + shifted(
            contract_cols(grad_right, w_right[tap_index]).reshape(group_shape), -offset
        )
    grad_w_right = jnp.stack(right_rows)
    grad_normed_branch = collect_rows(grad_branch_in) * valid_own[..., None]
    grad_resid, grad_gain_branch = normalize_back(
        grad_normed_branch, unit_branch, inv_branch, gain_branch
    )
    grad_one = grad_two + grad_resid
    grad_glu = lax.all_to_all(
        grad_one.astype(jnp.bfloat16), "mp", split_axis=2, concat_axis=1, tiled=True
    )
    grad_glu_flat = grad_glu.reshape(group_rows, -1).astype(jnp.float32)
    flat_glu = spread_rows(normed_glu.astype(jnp.bfloat16)).reshape(group_rows, model_width)
    value_pre = matmul(flat_glu, w_value)
    gate_sig = jax.nn.sigmoid(matmul(flat_glu, w_gate))
    grad_value = (grad_glu_flat * gate_sig).astype(jnp.bfloat16)
    grad_gate = (grad_glu_flat * value_pre * gate_sig * (1.0 - gate_sig)).astype(jnp.bfloat16)
    grad_w_value = contract_rows(flat_glu, grad_value)
    grad_w_gate = contract_rows(flat_glu, grad_gate)
    grad_glu_in = contract_cols(grad_value, w_value) + contract_cols(grad_gate, w_gate)
    grad_normed_glu = collect_rows(grad_glu_in.reshape(group_shape))
    grad_resid, grad_gain_glu = normalize_back(grad_normed_glu, unit_glu, inv_glu, gain_glu)
    grad_inputs = (grad_one + grad_resid).astype(jnp.bfloat16)
    gains = (grad_gain_glu, grad_gain_branch, grad_gain_attn, grad_gain_ffn)
    shards = (
        grad_w_value,
        grad_w_gate,
        grad_w_left,
        grad_w_right,
        grad_gain_mid,
        grad_w_depth,
        grad_w_point,
        grad_w_qkv,
        grad_w_out,
        grad_w_in,
        grad_w_back,
    )
    return (outputs, grad_inputs, gains, shards)


def local(
    inputs,
    lengths,
    gain_glu,
    w_value,
    w_gate,
    gain_branch,
    w_left,
    w_right,
    gain_mid,
    w_depth,
    w_point,
    gain_attn,
    w_qkv,
    w_out,
    gain_ffn,
    w_in,
    w_back,
    cotangent,
):
    outputs, grad_inputs, gains, shards = split_pass(
        inputs,
        lengths,
        gain_glu,
        w_value,
        w_gate,
        gain_branch,
        w_left,
        w_right,
        gain_mid,
        w_depth,
        w_point,
        gain_attn,
        w_qkv,
        w_out,
        gain_ffn,
        w_in,
        w_back,
        cotangent,
    )
    gain_totals = lax.psum((gains[0], gains[1], gains[2], gains[3]), ("dp", "mp"))
    weight_totals = (
        lax.psum(shards[0].astype(jnp.bfloat16), "dp").astype(jnp.float32),
        lax.psum(shards[1].astype(jnp.bfloat16), "dp").astype(jnp.float32),
        lax.psum(shards[2].astype(jnp.bfloat16), "dp").astype(jnp.float32),
        lax.psum(shards[3].astype(jnp.bfloat16), "dp").astype(jnp.float32),
        lax.psum(shards[4].astype(jnp.bfloat16), "dp").astype(jnp.float32),
        lax.psum(shards[5].astype(jnp.bfloat16), "dp").astype(jnp.float32),
        lax.psum(shards[6].astype(jnp.bfloat16), "dp").astype(jnp.float32),
        lax.psum(shards[7].astype(jnp.bfloat16), "dp").astype(jnp.float32),
        lax.psum(shards[8].astype(jnp.bfloat16), "dp").astype(jnp.float32),
        lax.psum(shards[9].astype(jnp.bfloat16), "dp").astype(jnp.float32),
        lax.psum(shards[10].astype(jnp.bfloat16), "dp").astype(jnp.float32),
    )
    return (
        outputs,
        grad_inputs,
        gain_totals[0],
        weight_totals[0],
        weight_totals[1],
        gain_totals[1],
        weight_totals[2],
        weight_totals[3],
        weight_totals[4],
        weight_totals[5],
        weight_totals[6],
        gain_totals[2],
        weight_totals[7],
        weight_totals[8],
        gain_totals[3],
        weight_totals[9],
        weight_totals[10],
    )


def solution(mesh):
    placed = (
        P("dp", "mp", None),
        P("dp"),
        P(),
        P(None, "mp"),
        P(None, "mp"),
        P(),
        P(None, "mp"),
        P(None, None, "mp"),
        P("mp"),
        P(None, "mp"),
        P("mp", None),
        P(),
        P(None, None, "mp"),
        P("mp", None),
        P(),
        P(None, "mp"),
        P("mp", None),
        P("dp", "mp", None),
    )
    return jax.shard_map(
        local,
        mesh=mesh,
        in_specs=placed,
        out_specs=(
            P("dp", "mp", None),
            P("dp", "mp", None),
            P(),
            P(None, "mp"),
            P(None, "mp"),
            P(),
            P(None, "mp"),
            P(None, None, "mp"),
            P("mp"),
            P(None, "mp"),
            P("mp", None),
            P(),
            P(None, None, "mp"),
            P("mp", None),
            P(),
            P(None, "mp"),
            P("mp", None),
        ),
        check_vma=False,
    )
```

profile of v0, /device:TPU:0, one launch (start us, length us, event | category | flops | bytes accessed | tf_op | source)
XLA Modules:
  0.0 694.9 jit_solution(1192619367773264075)
XLA Ops:
  12.0 24.2 %all-gather.7.cloned.1.call-done = bf16[1,1024,512]{2,1,0:T(8,128)(2,1)} async-done(((bf16[1,512,512]{2,1,0:T(8,128)(2,1)}), bf16[1,1024,512]{2,1,0:T(8,128)(2,1)}) %all-gather.7.cloned.1.call-update) | async-done | bytes 1048592 | tf_op jit(solution)/shard_map/all_gather | solution.py:33
  51.2 7.5 %all-to-all-done = bf16[2,2,65536]{2,1,0:T(2,128)(2,1)S(1)} async-done(((bf16[2,2,65536]{2,1,0:T(2,128)(2,1)}), bf16[2,2,65536]{2,1,0:T(2,128)(2,1)S(1)}, u32[]{:S(2)}, u32[]{:S(2)}) %all-to-all-start) | async-done | bytes 524320 | tf_op jit(solution)/shard_map/all_to_all | solution.py:232
  67.9 20.5 %all-gather.9.cloned.1.call-done = bf16[1,1024,512]{2,1,0:T(8,128)(2,1)} async-done(((bf16[1,512,512]{2,1,0:T(8,128)(2,1)}), bf16[1,1024,512]{2,1,0:T(8,128)(2,1)}) %all-gather.9.cloned.1.call-update) | async-done | bytes 1048592 | tf_op jit(solution)/shard_map/all_gather | solution.py:33
  101.9 7.2 %fusion.189 = (f32[1024]{0:T(1024)S(1)}, f32[1024]{0:T(1024)S(1)}, f32[1024,1024]{1,0:T(8,128)}, f32[1024,1024]{1,0:T(8,128)}) fusion(f32[1024,1024]{1,0:T(8,128)} %copy.62, bf16[512,1024]{1,0:T(8,128)(2,1)S(1)} %copy-done, bf16[1,1024,512]{2,1,0:T(8,128)(2,1)S(1)} %copy-done.7), kind=kOutput, calls=%fused_computation.311 | convolution fusion | flops 1082128384 | bytes 14688256 | tf_op jit(solution)/shard_map/dot_general | solution.py:17
  126.5 14.7 %reduce-scatter.8.cloned.1.call-done = bf16[1,512,256]{2,1,0:T(8,128)(2,1)} async-done(((bf16[1,1024,256]{2,1,0:T(8,128)(2,1)}), bf16[1,512,256]{2,1,0:T(8,128)(2,1)}) %reduce-scatter.8.cloned.1.call-update) | async-done | bytes 262160 | tf_op jit(solution)/shard_map/reduce_scatter | solution.py:37
  145.8 21.1 %all-gather.11.cloned.1.call-done = bf16[1,1024,512]{2,1,0:T(8,128)(2,1)} async-done(((bf16[1,512,512]{2,1,0:T(8,128)(2,1)}), bf16[1,1024,512]{2,1,0:T(8,128)(2,1)}) %all-gather.11.cloned.1.call-update) | async-done | bytes 1048592 | tf_op jit(solution)/shard_map/all_gather | solution.py:33
  183.4 20.4 %reduce-scatter.10.cloned.1.call-done = bf16[1,512,512]{2,1,0:T(8,128)(2,1)} async-done(((bf16[1,1024,512]{2,1,0:T(8,128)(2,1)}), bf16[1,512,512]{2,1,0:T(8,128)(2,1)}) %reduce-scatter.10.cloned.1.call-update) | async-done | bytes 524304 | tf_op jit(solution)/shard_map/reduce_scatter | solution.py:37
  207.7 20.2 %all-gather.13.cloned.1.call-done = bf16[1,1024,512]{2,1,0:T(8,128)(2,1)} async-done(((bf16[1,512,512]{2,1,0:T(8,128)(2,1)}), bf16[1,1024,512]{2,1,0:T(8,128)(2,1)}) %all-gather.13.cloned.1.call-update) | async-done | bytes 1048592 | tf_op jit(solution)/shard_map/all_gather | solution.py:33
  233.7 17.1 %all-gather.15.cloned.1.call-done = bf16[1,1024,512]{2,1,0:T(8,128)(2,1)} async-done(((bf16[1,512,512]{2,1,0:T(8,128)(2,1)}), bf16[1,1024,512]{2,1,0:T(8,128)(2,1)}) %all-gather.15.cloned.1.call-update) | async-done | bytes 1048592 | tf_op jit(solution)/shard_map/all_gather | solution.py:33
  263.5 16.3 %reduce-scatter.14.cloned.1.call-done = bf16[1,512,512]{2,1,0:T(8,128)(2,1)} async-done(((bf16[1,1024,512]{2,1,0:T(8,128)(2,1)}), bf16[1,512,512]{2,1,0:T(8,128)(2,1)}) %reduce-scatter.14.cloned.1.call-update) | async-done | bytes 524304 | tf_op jit(solution)/shard_map/reduce_scatter | solution.py:37
  281.4 21.6 %reduce-scatter.12.cloned.1.call-done = bf16[1,512,512]{2,1,0:T(8,128)(2,1)} async-done(((bf16[1,1024,512]{2,1,0:T(8,128)(2,1)}), bf16[1,512,512]{2,1,0:T(8,128)(2,1)}) %reduce-scatter.12.cloned.1.call-update) | async-done | bytes 524304 | tf_op jit(solution)/shard_map/reduce_scatter | solution.py:37
  306.5 21.2 %all-gather.17.cloned.1.call-done = bf16[1,1024,512]{2,1,0:T(8,128)(2,1)} async-done(((bf16[1,512,512]{2,1,0:T(8,128)(2,1)}), bf16[1,1024,512]{2,1,0:T(8,128)(2,1)}) %all-gather.17.cloned.1.call-update) | async-done | bytes 1048592 | tf_op jit(solution)/shard_map/all_gather | solution.py:33
  335.3 6.3 fusion.21
  341.7 10.7 %multiply_reduce_fusion = (f32[4,512]{1,0:T(4,128)S(1)}, f32[4,512]{1,0:T(4,128)S(1)}, f32[4,512,1024]{2,1,0:T(8,128)}) fusion(f32[4,512]{1,0:T(4,128)S(1)} %get-tuple-element.209, f32[4,512,1024]{2,1,0:T(8,128)} %copy-done.4, pred[1024]{0:T(1024)(128)(4,1)S(1)} %iota_compare_fusion, f32[4,512,1024]{2,1,0:T(8,128)} %fusion.201, ...), kind=kOutput, calls=%fused_computation.1 | convolution fusion | flops 289402880 | bytes 34374656 | tf_op jit(solution)/shard_map/while/body/eval_jaxpr/qhd,khd->hqk/dot_general | solution.py:119
  352.6 9.9 %multiply_convert_fusion = (bf16[4,512,1024]{2,1,0:T(8,128)(2,1)}, bf16[4,512,1024]{2,1,0:T(8,128)(2,1)S(1)}) fusion(f32[4,512,1024]{2,1,0:T(8,128)} %get-tuple-element.207, f32[4,512]{1,0:T(4,128)S(1)} %get-tuple-element.144, f32[4,512]{1,0:T(4,128)S(1)} %get-tuple-element.209, f32[4,512,1024]{2,1,0:T(8,128)S(1)} %bitcast.305, ...), kind=kLoop, calls=%fused_computation | loop fusion | flops 25165824 | bytes 41976832 | tf_op jit(solution)/shard_map/while/body/eval_jaxpr/convert_element_type | solution.py:123
  384.6 20.0 %reduce-scatter.16.cloned.1.call-done = bf16[1,512,512]{2,1,0:T(8,128)(2,1)} async-done(((bf16[1,1024,512]{2,1,0:T(8,128)(2,1)}), bf16[1,512,512]{2,1,0:T(8,128)(2,1)}) %reduce-scatter.16.cloned.1.call-update) | async-done | bytes 524304 | tf_op jit(solution)/shard_map/reduce_scatter | solution.py:37
  408.2 8.8 %all_gather.31 = bf16[1,1024,256]{2,1,0:T(8,128)(2,1)} all-gather(bf16[1,512,256]{2,1,0:T(8,128)(2,1)S(1)} %slice.402), channel_id=1, replica_groups=mesh['dp'=16,'mp'=2] {'mp'}, dimensions={1}, use_global_device_ids=true | all-gather | bytes 786432 | tf_op jit(solution)/shard_map/all_gather | solution.py:33
  417.1 6.0 multiply_reduce_fusion.2
  423.1 8.1 %fusion.28 = (bf16[1024]{0:T(1024)(128)(2,1)S(1)}, f32[1024]{0:T(1024)S(1)}, f32[1024]{0:T(1024)S(1)}, f32[1,1024,1024]{2,1,0:T(8,128)}) fusion(f32[1024]{0:T(1024)S(1)} %bitcast.339, f32[1024,1024]{1,0:T(8,128)S(1)} %copy-done.2, f32[1024]{0:T(1024)S(1)} %bitcast.344, f32[1024]{0:T(1024)S(1)} %convert_element_type.314, f32[1024]{0:T(1024)S(1)} %fusion.171, ...), kind=kLoop, calls=%fused_computation.59 | loop fusion | flops 27259904 | bytes 16840704 | tf_op jit(solution)/shard_map/reduce_sum | solution.py:309
  436.3 7.6 %fusion.25 = (bf16[1,1024,1024]{2,1,0:T(8,128)(2,1)}, f32[1,1024,1024]{2,1,0:T(8,128)}) fusion(f32[1024,1024]{1,0:T(8,128)} %get-tuple-element.201, f32[1024]{0:T(1024)S(1)} %bitcast.368, f32[1024]{0:T(1024)S(1)} %bitcast.340, f32[1024,1024]{1,0:T(8,128)} %get-tuple-element.176, f32[1024]{0:T(1024)S(1)} %bitcast.345, f32[1024]{0:T(1024)S(1)} %bitcast.369, ...), kind=kLoop, calls=%fused_computation.53 | loop fusion | flops 16777216 | bytes 18894848 | tf_op jit(solution)/shard_map/convert_element_type | solution.py:316
  462.9 13.8 %reduce-scatter.18.cloned.1.call-done = bf16[1,512,512]{2,1,0:T(8,128)(2,1)} async-done(((bf16[1,1024,512]{2,1,0:T(8,128)(2,1)}), bf16[1,512,512]{2,1,0:T(8,128)(2,1)}) %reduce-scatter.18.cloned.1.call-update) | async-done | bytes 524304 | tf_op jit(solution)/shard_map/reduce_scatter | solution.py:37
  524.0 62.4 %all-reduce.25 = (bf16[1024]{0:T(1024)(128)(2,1)S(1)}, bf16[9,1024]{1,0:T(8,128)(2,1)S(1)}) all-reduce(bf16[1024]{0:T(1024)(128)(2,1)S(1)} %get-tuple-element.119, bf16[9,1024]{1,0:T(8,128)(2,1)S(1)} %stack.82), channel_id=1, replica_groups=mesh['dp'=16,'mp'=2] {'dp'}, use_global_device_ids=true, to_apply=%region_46.47 | all-reduce | flops 10240 | bytes 40960 | tf_op jit(solution)/shard_map/psum | solution.py:419
  589.3 37.3 %all-reduce.22 = (f32[512]{0:T(512)}, f32[512]{0:T(512)}, f32[512]{0:T(512)}, f32[512]{0:T(512)}) all-reduce(f32[512]{0:T(512)S(1)} %get-tuple-element.138, f32[512]{0:T(512)S(1)} %get-tuple-element.134, f32[512]{0:T(512)S(1)} %get-tuple-element.132, f32[512]{0:T(512)S(1)} %get-tuple-element.136), channel_id=1, replica_groups=mesh['dp'=16,'mp'=2] {'dp','mp'}, use_global_device_ids=true, to_apply=%region_38.39 | all-reduce | flops 2048 | bytes 16384 | tf_op jit(solution)/shard_map/psum | solution.py:413
  628.9 42.1 %all-reduce.29.cloned.1.call-done = (bf16[3,512,256]{1,2,0:T(8,128)(2,1)}, bf16[512,256]{1,0:T(8,128)(2,1)}, bf16[512,256]{1,0:T(8,128)(2,1)}, bf16[512,1024]{1,...) async-done(((bf16[3,512,256]{1,2,0:T(8,128)(2,1)}, ...) | async-done | bytes 5636112 | tf_op jit(solution)/shard_map/psum | solution.py:422
  (354 shorter events, 233.7 us)
Async XLA Ops:
  7.2 94.7 %copy-start = (bf16[512,1024]{1,0:T(8,128)(2,1)S(1)}, bf16[512,1024]{1,0:T(8,128)(2,1)}, u32[]{:S(2)}) copy-start(bf16[512,1024]{1,0:T(8,128)(2,1)} %param.24) | copy-start | bytes 3145732
  7.2 30.8 %copy-start.46 = (bf16[512,256]{1,0:T(8,128)(2,1)S(1)}, bf16[512,256]{1,0:T(8,128)(2,1)}, u32[]{:S(2)}) copy-start(bf16[512,256]{1,0:T(8,128)(2,1)} %param.21) | copy-start | bytes 786436
  7.2 29.0 %all-gather.7.cloned.1.call-start = ((), (), s32[]{:S(2)}) async-start(), calls=%async_computation.9 | async-start | bytes 1572864 | tf_op jit(solution)/shard_map/all_gather | solution.py:33
  47.0 11.7 %all-to-all-start = ((bf16[2,2,65536]{2,1,0:T(2,128)(2,1)}), bf16[2,2,65536]{2,1,0:T(2,128)(2,1)S(1)}, u32[]{:S(2)}, u32[]{:S(2)}) async-start(bf16[2,2,65536]{2,1,0:T(2,128)(2,1)} %reshape.550), calls=%async_computation | async-start | bytes 1048576 | tf_op jit(solution)/shard_map/all_to_all | solution.py:232
  50.5 37.9 %all-gather.9.cloned.1.call-start = ((), (), s32[]{:S(2)}) async-start(), calls=%async_computation.10 | async-start | bytes 1572864 | tf_op jit(solution)/shard_map/all_gather | solution.py:33
  67.0 74.1 %reduce-scatter.8.cloned.1.call-start = ((), (), s32[]{:S(2)}) async-start(), calls=%async_computation.11 | async-start | bytes 786432 | tf_op jit(solution)/shard_map/reduce_scatter | solution.py:37
  126.4 40.5 %copy-start.82 = (bf16[3,512,256]{2,1,0:T(8,128)(2,1)S(1)}, bf16[3,512,256]{2,1,0:T(8,128)(2,1)}, u32[]{:S(2)}) copy-start(bf16[3,512,256]{2,1,0:T(8,128)(2,1)} %param.30) | copy-start | bytes 2359300
  126.4 40.5 %all-gather.11.cloned.1.call-start = ((), (), s32[]{:S(2)}) async-start(), calls=%async_computation.12 | async-start | bytes 1572864 | tf_op jit(solution)/shard_map/all_gather | solution.py:33
  145.4 58.4 %reduce-scatter.10.cloned.1.call-start = ((), (), s32[]{:S(2)}) async-start(), calls=%async_computation.13 | async-start | bytes 1572864 | tf_op jit(solution)/shard_map/reduce_scatter | solution.py:37
  183.4 44.5 %all-gather.13.cloned.1.call-start = ((), (), s32[]{:S(2)}) async-start(), calls=%async_computation.14 | async-start | bytes 1572864 | tf_op jit(solution)/shard_map/all_gather | solution.py:33
  206.4 44.4 %all-gather.15.cloned.1.call-start = ((), (), s32[]{:S(2)}) async-start(), calls=%async_computation.16 | async-start | bytes 1572864 | tf_op jit(solution)/shard_map/all_gather | solution.py:33
  207.2 72.6 %reduce-scatter.14.cloned.1.call-start = ((), (), s32[]{:S(2)}) async-start(), calls=%async_computation.17 | async-start | bytes 1572864 | tf_op jit(solution)/shard_map/reduce_scatter | solution.py:37
  259.3 43.7 %reduce-scatter.12.cloned.1.call-start = ((), (), s32[]{:S(2)}) async-start(), calls=%async_computation.15 | async-start | bytes 1572864 | tf_op jit(solution)/shard_map/reduce_scatter | solution.py:37
  263.4 64.2 %all-gather.17.cloned.1.call-start = ((), (), s32[]{:S(2)}) async-start(), calls=%async_computation.18 | async-start | bytes 1572864 | tf_op jit(solution)/shard_map/all_gather | solution.py:33
  306.2 98.4 %reduce-scatter.16.cloned.1.call-start = ((), (), s32[]{:S(2)}) async-start(), calls=%async_computation.19 | async-start | bytes 1572864 | tf_op jit(solution)/shard_map/reduce_scatter | solution.py:37
  384.1 92.6 %reduce-scatter.18.cloned.1.call-start = ((), (), s32[]{:S(2)}) async-start(), calls=%async_computation.20 | async-start | bytes 1572864 | tf_op jit(solution)/shard_map/reduce_scatter | solution.py:37
  488.4 12.6 %all-to-all-start.1 = ((bf16[2,2,65536]{2,1,0:T(2,128)(2,1)}), bf16[2,2,65536]{2,1,0:T(2,128)(2,1)}, u32[]{:S(2)}, u32[]{:S(2)}) async-start(bf16[2,2,65536]{2,1,0:T(2,128)(2,1)} %reshape.552), calls=%async_computation.7 | async-start | bytes 1048576 | tf_op jit(solution)/shard_map/all_to_all | solution.py:341
  492.6 95.0 %reduce-scatter.20.cloned.1.call-start = ((), (), s32[]{:S(2)}) async-start(), calls=%async_computation.21 | async-start | bytes 1572864 | tf_op jit(solution)/shard_map/reduce_scatter | solution.py:37
  508.3 162.7 %all-reduce.29.cloned.1.call-start = ((), (), s32[]{:S(2)}) async-start(), calls=%async_computation.22 | async-start | bytes 11272192 | tf_op jit(solution)/shard_map/psum | solution.py:422
  519.6 68.0 %copy-start.10 = (bf16[1,512,512]{2,1,0:T(8,128)(2,1)S(1)}, bf16[1,512,512]{2,1,0:T(8,128)(2,1)}, u32[]{:S(2)}) copy-start(bf16[1,512,512]{2,1,0:T(8,128)(2,1)} %param.18) | copy-start | bytes 1572868
  519.6 68.0 %copy-start.60 = (f32[512]{0:T(512)S(1)}, f32[512]{0:T(512)}, u32[]{:S(2)}) copy-start(f32[512]{0:T(512)} %copy-done.59) | copy-start | bytes 6148
  519.6 68.0 %copy-start.74 = (f32[512]{0:T(512)S(1)}, f32[512]{0:T(512)}, u32[]{:S(2)}) copy-start(f32[512]{0:T(512)} %copy-done.73) | copy-start | bytes 6148
  519.7 68.0 %copy-start.79 = (f32[512]{0:T(512)S(1)}, f32[512]{0:T(512)}, u32[]{:S(2)}) copy-start(f32[512]{0:T(512)} %param.20) | copy-start | bytes 6148
  519.7 107.0 %copy-start.25 = (f32[1,512,512]{2,1,0:T(8,128)S(1)}, f32[1,512,512]{2,1,0:T(8,128)}, u32[]{:S(2)}) copy-start(f32[1,512,512]{2,1,0:T(8,128)} %get-tuple-element.168) | copy-start | bytes 3145732
  (81 other events, 618.7 us)
Sparse Core Ops, SparseCore 0:
  12.2 23.9 all-gather.6
  67.1 21.2 all-gather.8
  126.5 14.5 reduce-scatter.7
  145.6 21.2 all-gather.10
  183.5 20.3 reduce-scatter.9
  206.5 21.3 all-gather.12
  229.4 21.2 all-gather.14
  259.4 20.3 reduce-scatter.13
  282.7 20.3 reduce-scatter.11
  306.3 21.2 all-gather.16
  384.3 20.3 reduce-scatter.15
  456.4 20.3 reduce-scatter.17
  508.4 20.3 reduce-scatter.19
  536.0 134.9 all-reduce.28
where the time goes:
time: 703 us; the launch traced here: 695 us
  waiting for transfers between devices  286 us (41%)
  matrix products  118 us (17%)
  blocking collectives  118 us (17%)
  other arithmetic  99.1 us (14%)
  local copies, waits for them, and re-layouts  47.4 us (7%)
  between operations  16 us (2%)
  starting transfers between devices  9.96 us (1%)
    all_gather x6, waiting for transfers between devices, spread_rows(): return lax.all_gather(pieces, 'mp', axis=1, tiled=True)  124 us
    reduce_scatter x7, waiting for transfers between devices, collect_rows(): lax.psum_scatter(partial_value.astype(jnp.bfloat16), 'mp', scatter_dimens...  107 us
    psum x1, blocking collectives, local(): lax.psum(shards[4].astype(jnp.bfloat16), 'dp').astype(jnp.float32)  62.4 us
    psum x1, waiting for transfers between devices, local(): lax.psum(shards[7].astype(jnp.bfloat16), 'dp').astype(jnp.float32)  42.1 us
    psum x1, blocking collectives, local(): lax.psum((gains[0], gains[1], gains[2], gains[3]), ('dp', 'mp'))  37.3 us
    dot_general x10, matrix products, matmul(): return jnp.dot(left_side, right_side, preferred_element_type=jnp.float32)  26.2 us
    dot_general x10, matrix products, contract_cols(): lax.dot_general(left_side, right_side, (((1,), (1,)), ((), ())), preferre...  20.8 us
    dot_general x10, matrix products, contract_rows(): lax.dot_general(left_side, right_side, (((0,), (0,)), ((), ())), preferre...  16.9 us
  transfers between devices with their start and end apart: 16, of which 15 were waited for; matrix products, arithmetic and copies ran while one was open for 6% of the time, Pallas kernels for 0%

commit v1 on v0

--- a/solution.py
+++ b/solution.py
@@ -7,6 +7,7 @@
 
 FF = 2048
 HEAD_DIM = 64
+EDGE = 16
 
 
 epsilon = 1e-06
@@ -445,6 +446,295 @@
     )
 
 
+def other_core(dp_size):
+    return [(index, index ^ 1) for index in range(dp_size)]
+
+
+def over_mp(values):
+    return lax.ppermute(values, "mp", [(0, 1), (1, 0)])
+
+
+def over_core(values):
+    return lax.ppermute(values, "dp", other_core(lax.axis_size("dp")))
+
+
+def flat_pairs(dp_size, rule):
+    pairs = []
+    for dp_index in range(dp_size):
+        for member in range(2):
+            pair, core = dp_index // 2, dp_index % 2
+            new_core, new_member = rule(core, member)
+            pairs.append((dp_index * 2 + member, (pair * 2 + new_core) * 2 + new_member))
+    return pairs
+
+
+def swap_blocks(values, member, core):
+    pairs = flat_pairs(lax.axis_size("dp"), lambda c, m: (m, c))
+    pairs = [pair for pair in pairs if pair[0] != pair[1]]
+    moved = lax.ppermute(values, ("dp", "mp"), pairs)
+    return jnp.where(member == core, values, moved)
+
+
+def edge_rows(values, member, core):
+    rows = values.shape[0]
+    edge = jnp.where(member == 0, values[rows - EDGE :], values[:EDGE])
+    pairs = flat_pairs(lax.axis_size("dp"), lambda c, m: (1 - m, c))
+    return lax.ppermute(edge, ("dp", "mp"), pairs)
+
+
+def with_edges(values, edge, core):
+    blank = jnp.zeros_like(edge)
+    before = jnp.where(core == 1, edge, blank)
+    after = jnp.where(core == 1, blank, edge)
+    return jnp.concatenate([before, values, after], axis=0)
+
+
+def partner_half(weight, core):
+    half = weight.shape[0] // 2
+    got = over_mp(lax.dynamic_slice_in_dim(weight, core * half, half, axis=0))
+    part = over_core(got)
+    return jnp.where(
+        core == 0, jnp.concatenate([got, part], axis=0), jnp.concatenate([part, got], axis=0)
+    )
+
+
+def norm_rows(values, gain_vec):
+    centre = values - jnp.mean(values, axis=-1, keepdims=True)
+    scale_inv = lax.rsqrt(jnp.mean(centre * centre, axis=-1, keepdims=True) + epsilon)
+    unit_rows = centre * scale_inv
+    return (unit_rows * gain_vec, unit_rows, scale_inv)
+
+
+def norm_rows_back(grad_out, unit_rows, scale_inv, gain_vec):
+    scaled = grad_out * gain_vec
+    mean_one = jnp.mean(scaled, axis=-1, keepdims=True)
+    mean_two = jnp.mean(scaled * unit_rows, axis=-1, keepdims=True)
+    grad_in = scale_inv * (scaled - mean_one - unit_rows * mean_two)
+    return (grad_in, jnp.sum(grad_out * unit_rows, axis=0))
+
+
+def roll_rows(values, offset):
+    if offset == 0:
+        return values
+    return jnp.roll(values, -offset, axis=0)
+
+
+def paired(
+    inputs, lengths, gain_glu, w_value, w_gate, gain_branch, w_left, w_right, gain_mid, w_depth,
+    w_point, gain_attn, w_qkv, w_out, gain_ffn, w_in, w_back, cotangent,
+):
+    low = jnp.bfloat16
+    member = lax.axis_index("mp")
+    core = lax.axis_index("dp") % 2
+    rows, width = inputs.shape[1:]
+    own = slice(EDGE, EDGE + rows)
+
+    length = swap_blocks(lengths, member, core)[0]
+    edge = edge_rows(inputs[0], member, core)
+    block = swap_blocks(inputs[0], member, core)
+    cot = swap_blocks(cotangent[0], member, core)
+
+    def both(weight, axis):
+        return jnp.concatenate([weight, partner_half(weight, core)], axis=axis)
+
+    def ordered(weight, axis):
+        other = partner_half(weight, core)
+        return jnp.where(
+            member == 0,
+            jnp.concatenate([weight, other], axis=axis),
+            jnp.concatenate([other, weight], axis=axis),
+        )
+
+    value_w = ordered(w_value, 1)
+    gate_w = ordered(w_gate, 1)
+    left_w = both(w_left, 1)
+    right_w = jnp.concatenate(
+        [w_right, partner_half(w_right.reshape(-1, w_right.shape[2]), core).reshape(w_right.shape)],
+        axis=2,
+    )
+    mid_gain = jnp.concatenate([gain_mid, over_mp(gain_mid)]).astype(jnp.float32)
+    taps = jnp.concatenate([w_depth, over_mp(w_depth)], axis=1).astype(jnp.float32)
+    point_w = both(w_point, 0)
+    qkv_w = jnp.concatenate(
+        [w_qkv, partner_half(w_qkv.reshape(-1, w_qkv.shape[2]), core).reshape(w_qkv.shape)], axis=2
+    )
+    out_w = both(w_out, 0)
+    in_w = both(w_in, 1)
+    back_w = both(w_back, 0)
+    inner = left_w.shape[1]
+    right_cols = right_w.shape[2]
+    stride = inner // right_cols
+    sep_width = point_w.shape[1]
+    sep_taps = taps.shape[0]
+    conv_taps = right_w.shape[0]
+    heads = qkv_w.shape[2] // HEAD_DIM
+    score_scale = 1.0 / math.sqrt(HEAD_DIM)
+
+    positions = core * rows - EDGE + jnp.arange(rows + 2 * EDGE)
+    valid = ((positions >= 0) & (positions < length)).astype(jnp.float32)[:, None]
+
+    resid_in = with_edges(block, edge, core).astype(jnp.float32)
+    normed, unit_glu, inv_glu = norm_rows(resid_in, gain_glu)
+    glu_in = normed.astype(low)
+    value_pre = matmul(glu_in, value_w)
+    gate_sig = jax.nn.sigmoid(matmul(glu_in, gate_w))
+    glu_out = (value_pre * gate_sig).astype(low)
+    resid_one = resid_in + glu_out.astype(jnp.float32)
+    normed, unit_branch, inv_branch = norm_rows(resid_one, gain_branch)
+    branch_in = (valid * normed).astype(low)
+    left_pre = matmul(branch_in, left_w)
+    right_pre = sum(
+        matmul(roll_rows(branch_in, tap - conv_taps // 2), right_w[tap]) for tap in range(conv_taps)
+    )
+    spread = (
+        jnp.arange(inner)[None, :] == stride * jnp.arange(right_cols)[:, None]
+    ).astype(low)
+    mid = jax.nn.silu(left_pre) + matmul(jax.nn.silu(right_pre).astype(low), spread)
+    mid_mean = jnp.mean(mid, axis=-1, keepdims=True)
+    inv_mid = lax.rsqrt(jnp.mean((mid - mid_mean) ** 2, axis=-1, keepdims=True) + epsilon)
+    unit_mid = (mid - mid_mean) * inv_mid
+    depth_in = valid * unit_mid * mid_gain
+    depth = sum(
+        roll_rows(depth_in, tap - sep_taps // 2)[own] * taps[tap] for tap in range(sep_taps)
+    ).astype(low)
+    sep_rows = matmul(depth, point_w)
+    resid_two = resid_one[own] + jnp.pad(sep_rows, ((0, 0), (0, width - sep_width)))
+    normed, unit_attn, inv_attn = norm_rows(resid_two, gain_attn)
+    attn_in = normed.astype(low)
+    qkv = [matmul(attn_in, qkv_w[index]).astype(low) for index in range(3)]
+    kv_own = jnp.concatenate(qkv[1:], axis=1)
+    kv_far = over_core(kv_own)
+    kv_all = jnp.where(
+        core == 0,
+        jnp.concatenate([kv_own, kv_far], axis=0),
+        jnp.concatenate([kv_far, kv_own], axis=0),
+    )
+    key_valid = jnp.arange(2 * rows) < length
+    queries = qkv[0].reshape(rows, heads, HEAD_DIM)
+    keys = kv_all[:, : heads * HEAD_DIM].reshape(2 * rows, heads, HEAD_DIM)
+    vals = kv_all[:, heads * HEAD_DIM :].reshape(2 * rows, heads, HEAD_DIM)
+    context, log_sums = attend_forward(queries, keys, vals, key_valid, rows, score_scale)
+    context_low = context.astype(low).reshape(rows, heads * HEAD_DIM)
+    resid_three = resid_two + matmul(context_low, out_w)
+    normed, unit_ffn, inv_ffn = norm_rows(resid_three, gain_ffn)
+    ffn_in = normed.astype(low)
+    ffn_pre = matmul(ffn_in, in_w)
+    ffn_hidden = jax.nn.silu(ffn_pre).astype(low)
+    outputs = (resid_three + matmul(ffn_hidden, back_w)).astype(low)
+    outputs = swap_blocks(outputs, member, core)
+
+    grad_hidden = contract_cols(cot, back_w)
+    grad_ffn_pre = (grad_hidden * silu_slope(ffn_pre)).astype(low)
+    grad_w_back = contract_rows(ffn_hidden, cot)
+    grad_w_in = contract_rows(ffn_in, grad_ffn_pre)
+    grad_resid, grad_gain_ffn = norm_rows_back(
+        contract_cols(grad_ffn_pre, in_w), unit_ffn, inv_ffn, gain_ffn
+    )
+    grad_three = cot.astype(jnp.float32) + grad_resid
+    grad_attn = grad_three.astype(low)
+    grad_w_out = contract_rows(context_low, grad_attn)
+    grad_context = contract_cols(grad_attn, out_w).astype(low).reshape(queries.shape)
+    grad_q, grad_k, grad_v = attend_back(
+        queries, keys, vals, key_valid, log_sums, grad_context, rows, score_scale
+    )
+    grad_kv = jnp.concatenate([grad_k.reshape(2 * rows, -1), grad_v.reshape(2 * rows, -1)], axis=1)
+    kept = lax.dynamic_slice_in_dim(grad_kv, core * rows, rows, axis=0)
+    sent = lax.dynamic_slice_in_dim(grad_kv, (1 - core) * rows, rows, axis=0)
+    grad_kv = (kept + over_core(sent.astype(low)).astype(jnp.float32)).astype(low)
+    grad_qkv = jnp.stack(
+        [
+            grad_q.reshape(rows, -1),
+            grad_kv[:, : heads * HEAD_DIM],
+            grad_kv[:, heads * HEAD_DIM :],
+        ]
+    )
+    grad_w_qkv = jnp.stack([contract_rows(attn_in, grad_qkv[index]) for index in range(3)])
+    grad_attn_in = sum(contract_cols(grad_qkv[index], qkv_w[index]) for index in range(3))
+    grad_resid, grad_gain_attn = norm_rows_back(grad_attn_in, unit_attn, inv_attn, gain_attn)
+    grad_two = grad_three + grad_resid
+    grad_sep = grad_two[:, :sep_width].astype(low)
+    sep_edge = over_core(jnp.where(core == 0, grad_sep[rows - EDGE :], grad_sep[:EDGE]))
+    grad_sep_all = with_edges(grad_sep, sep_edge, core)
+    grad_w_point = contract_rows(depth, grad_sep)
+    grad_depth = contract_cols(grad_sep_all, point_w)
+    grad_depth_in = sum(
+        roll_rows(grad_depth, sep_taps // 2 - tap) * taps[tap] for tap in range(sep_taps)
+    )
+    grad_w_depth = jnp.stack(
+        [
+            jnp.sum(roll_rows(depth_in, tap - sep_taps // 2)[own] * grad_depth[own], axis=0)
+            for tap in range(sep_taps)
+        ]
+    )
+    grad_unit = grad_depth_in * valid
+    grad_gain_mid = jnp.sum((grad_unit * unit_mid)[own], axis=0)
+    scaled = grad_unit * mid_gain
+    grad_mid = inv_mid * (
+        scaled
+        - jnp.mean(scaled, axis=-1, keepdims=True)
+        - unit_mid * jnp.mean(scaled * unit_mid, axis=-1, keepdims=True)
+    )
+    grad_left = (grad_mid * silu_slope(left_pre)).astype(low)
+    grad_right = (contract_cols(grad_mid.astype(low), spread) * silu_slope(right_pre)).astype(low)
+    grad_w_left = contract_rows(branch_in[own], grad_left[own])
+    grad_branch_in = contract_cols(grad_left[own], left_w)
+    right_rows = []
+    for tap in range(conv_taps):
+        offset = tap - conv_taps // 2
+        right_rows.append(contract_rows(roll_rows(branch_in, offset)[own], grad_right[own]))
+        grad_branch_in = grad_branch_in + contract_cols(
+            roll_rows(grad_right, -offset)[own], right_w[tap]
+        )
+    grad_w_right = jnp.stack(right_rows)
+    grad_resid, grad_gain_branch = norm_rows_back(
+        grad_branch_in * valid[own], unit_branch[own], inv_branch[own], gain_branch
+    )
+    grad_one = grad_two + grad_resid
+    grad_glu = grad_one.astype(low).astype(jnp.float32)
+    sig = gate_sig[own]
+    grad_value = (grad_glu * sig).astype(low)
+    grad_gate = (grad_glu * value_pre[own] * sig * (1.0 - sig)).astype(low)
+    grad_w_value = contract_rows(glu_in[own], grad_value)
+    grad_w_gate = contract_rows(glu_in[own], grad_gate)
+    grad_resid, grad_gain_glu = norm_rows_back(
+        contract_cols(grad_value, value_w) + contract_cols(grad_gate, gate_w),
+        unit_glu[own], inv_glu[own], gain_glu,
+    )
+    grad_inputs = swap_blocks((grad_one + grad_resid).astype(low), member, core)
+
+    gain_totals = lax.psum(
+        (grad_gain_glu, grad_gain_branch, grad_gain_attn, grad_gain_ffn), ("dp", "mp")
+    )
+
+    def total(grad, axis, in_order=False):
+        half = grad.shape[axis] // 2
+        at = member if in_order else 0
+        mine = lax.dynamic_slice_in_dim(grad, at * half, half, axis=axis)
+        theirs = lax.dynamic_slice_in_dim(grad, (1 - at) * half, half, axis=axis)
+        mine = mine + over_mp(theirs.astype(low)).astype(jnp.float32)
+        return lax.psum(mine.astype(low), "dp").astype(jnp.float32)
+
+    return (
+        outputs[None],
+        grad_inputs[None],
+        gain_totals[0],
+        total(grad_w_value, 1, True),
+        total(grad_w_gate, 1, True),
+        gain_totals[1],
+        total(grad_w_left, 1),
+        total(grad_w_right, 2),
+        total(grad_gain_mid, 0),
+        total(grad_w_depth, 1),
+        total(grad_w_point, 0),
+        gain_totals[2],
+        total(grad_w_qkv, 2),
+        total(grad_w_out, 0),
+        gain_totals[3],
+        total(grad_w_in, 1),
+        total(grad_w_back, 0),
+    )
+
+
 def solution(mesh):
     placed = (
         P("dp", "mp", None),
@@ -466,8 +756,10 @@
         P("mp", None),
         P("dp", "mp", None),
     )
+    mp_size, dp_size = mesh.shape["mp"], mesh.shape["dp"]
+    plan = paired if mp_size == 2 and dp_size % 2 == 0 else local
     return jax.shard_map(
-        local,
+        plan,
         mesh=mesh,
         in_specs=placed,
         out_specs=(

time: 703 us -> 525 us (0.75)
  waiting for transfers between devices: 286 us -> 112 us
  starting transfers between devices: 9.96 us -> 51.4 us
  matrix products: 118 us -> 79 us
  other arithmetic: 99.1 us -> 120 us
  blocking collectives: 118 us -> 101 us
  local copies, waits for them, and re-layouts: 47.4 us -> 36.8 us
    all_gather x6 -> x0, waiting for transfers between devices: 124 us -> none  [spread_rows(): return lax.all_gather(pieces, 'mp', axis=1, tiled=True)]
    reduce_scatter x7 -> x0, waiting for transfers between devices: 107 us -> none  [collect_rows(): lax.psum_scatter(partial_value.astype(jnp.bfloat16), 'mp', scatter_dimens...]
    ppermute x0 -> x40, waiting for transfers between devices: none -> 102 us  [the longest x22 101 us: over_mp(): return lax.ppermute(values, 'mp', [(0, 1), (1, 0)])]
    ppermute x0 -> x40, starting transfers between devices: none -> 51.4 us  [the longest x22 31 us: over_mp(): return lax.ppermute(values, 'mp', [(0, 1), (1, 0)])]
    psum x1, waiting for transfers between devices: 42.1 us -> 9.69 us  [total(): return lax.psum(mine.astype(low), 'dp').astype(jnp.float32)]
    select_n x0 -> x16, other arithmetic: none -> 20.8 us  [the longest x1 10.3 us: paired(): jnp.where(core == 0, jnp.concatenate([kv_own, kv_far], axis=0), jnp.conca...]
    slice x6 -> x15, local copies, waits for them, and re-layouts: 3.47 us -> 17.2 us  [the longest x10 15 us: roll_rows(): return jnp.roll(values, -offset, axis=0)]
    dynamic_slice x0 -> x18, local copies, waits for them, and re-layouts: none -> 12.9 us  [the longest x9 10.4 us: partner_half(): got = over_mp(lax.dynamic_slice_in_dim(weight, core * half, half, axis=0))]
  transfers between devices with their start and end apart: 16 -> 41, of which waited for: 15 -> 12; matrix products, arithmetic and copies ran while one was open for 6% -> 27% of each run, Pallas kernels for 0% -> 0%
where the time goes in v1:
time: 525 us; the launch traced here: 519 us
  other arithmetic  120 us (23%)
  waiting for transfers between devices  112 us (21%)
  blocking collectives  101 us (19%)
  matrix products  79 us (15%)
  starting transfers between devices  51.4 us (10%)
  local copies, waits for them, and re-layouts  36.8 us (7%)
  between operations  17.7 us (3%)
    ppermute x22, waiting for transfers between devices, over_mp(): return lax.ppermute(values, 'mp', [(0, 1), (1, 0)])  101 us
    psum x1, blocking collectives, total(): return lax.psum(mine.astype(low), 'dp').astype(jnp.float32)  61.1 us
    psum x1, blocking collectives, paired(): lax.psum((grad_gain_glu, grad_gain_branch, grad_gain_attn, grad_gain_ffn)...  40.4 us
    ppermute x22, starting transfers between devices, over_mp(): return lax.ppermute(values, 'mp', [(0, 1), (1, 0)])  31 us
    convert_element_type x22, other arithmetic, total(): return lax.psum(mine.astype(low), 'dp').astype(jnp.float32)  28.6 us
    dot_general x14, matrix products, contract_cols(): lax.dot_general(left_side, right_side, (((1,), (1,)), ((), ())), preferre...  18 us
    reduce_sum x1, other arithmetic, paired(): jnp.sum(roll_rows(depth_in, tap - sep_taps // 2)[own] * grad_depth[own],...  17.7 us
    dot_general x14, matrix products, matmul(): return jnp.dot(left_side, right_side, preferred_element_type=jnp.float32)  15.4 us
  transfers between devices with their start and end apart: 41, of which 12 were waited for; matrix products, arithmetic and copies ran while one was open for 27% of the time, Pallas kernels for 0%

profile of v1, /device:TPU:0, one launch (start us, length us, event | category | flops | bytes accessed | tf_op | source)
XLA Modules:
  0.0 518.5 jit_solution(7608580537890592899)
XLA Ops:
  36.8 4.3 collective-permute-done.9
  46.1 17.5 %collective-permute-done.13 = bf16[512,256]{1,0:T(8,128)(2,1)S(1)} collective-permute-done((bf16[512,256]{1,0:T(8,128)(2,1)S(1)}, bf16[512,256]{1,0:T(8,128)(2,1)S(1)}, u32[]{:S(2)}, u32[]{:S(2)}) %collective-permute-start.13) | collective-permute-done | bytes 262176 | tf_op jit(solution)/shard_map/ppermute | solution.py:454
  73.3 12.9 %collective-permute-done.7 = bf16[256,1024]{1,0:T(8,128)(2,1)S(1)} collective-permute-done((bf16[256,1024]{1,0:T(8,128)(2,1)S(1)}, bf16[256,1024]{1,0:T(8,128)(2,1)S(1)}, u32[]{:S(2)}, u32[]{:S(2)}) %collective-permute-start.7) | collective-permute-done | bytes 524320 | tf_op jit(solution)/shard_map/ppermute | solution.py:454
  100.1 4.8 add_convert_fusion
  119.8 10.3 %maximum_select_fusion = bf16[1024,1024]{0,1:T(8,128)(2,1)S(1)} fusion(bf16[512,1024]{0,1:T(8,128)(2,1)} %collective-permute-done.17, bf16[512,512]{0,1:T(8,128)(2,1)S(1)} %copy-done.26, bf16[512,512]{0,1:T(8,128)(2,1)S(1)} %copy-done.28, pred[]{:T(512)S(6)} %eq.25), kind=kLoop, calls=%fused_computation.79 | loop fusion | flops 13631488 | bytes 4194305 | tf_op jit(solution)/shard_map/jit(_where)/select_n | solution.py:607
  137.0 4.9 fusion.46
  162.9 4.9 fusion.2
  167.8 10.9 %multiply_reduce_fusion = (f32[8,512]{1,0:T(8,128)}, f32[8,512,1024]{2,1,0:T(8,128)}) fusion(f32[8,512]{1,0:T(8,128)S(1)} %log_add_fusion, f32[8,512,1024]{2,1,0:T(8,128)S(1)} %get-tuple-element.109, pred[1024]{0:T(1024)(128)(4,1)} %copy-done.107, bf16[512,8,64]{0,2,1:T(8,128)(2,1)} %bitcast.161, bf16[1024,8,64]{0,2,1:T(8,128)(2,1)} %bitcast.155), kind=kOutput, calls=%fused_computation.1 | convolution fusion | flops 557838336 | bytes 35161088 | tf_op jit(solution)/shard_map/qhd,khd->hqk/dot_general | solution.py:120
  178.7 10.8 %multiply_convert_fusion = bf16[8,512,1024]{2,1,0:T(8,128)(2,1)} fusion(f32[8,512,1024]{2,1,0:T(8,128)} %get-tuple-element.116, f32[8,512]{1,0:T(8,128)} %get-tuple-element.115, f32[8,512]{1,0:T(8,128)S(1)} %log_add_fusion, f32[8,512,1024]{2,1,0:T(8,128)S(1)} %get-tuple-element.109, pred[1024]{0:T(1024)(128)(4,1)} %copy-done.107), kind=kLoop, calls=%fused_computation | loop fusion | flops 25165824 | bytes 41976832 | tf_op jit(solution)/shard_map/convert_element_type | solution.py:124
  189.5 6.5 %fusion.44 = bf16[8,64,512]{2,1,0:T(8,128)(2,1)S(1)} fusion(bf16[1024,8,64]{0,2,1:T(8,128)(2,1)} %bitcast.147, bf16[8,512,1024]{2,1,0:T(8,128)(2,1)} %multiply_convert_fusion), kind=kOutput, calls=%fused_computation.121 | convolution fusion | flops 537395200 | bytes 9961472 | tf_op jit(solution)/shard_map/hqk,khd->qhd/dot_general | solution.py:126
  215.0 10.3 %collective-permute-start.27 = (bf16[16,256]{1,0:T(8,128)(2,1)S(1)}, bf16[16,256]{1,0:T(8,128)(2,1)S(1)}, u32[]{:S(2)}, u32[]{:S(2)}) collective-permute-start(bf16[16,256]{1,0:T(8,128)(2,1)S(1)} %slice_select_fusion), channel_id=1, source_target_pairs={{0,2},{2,0},{4,6},{6,4},{8,10},{10,8},{12,14},{14,12},{16,18},{18,... | collective-permute-start | bytes 24584 | tf_op jit(solution)/shard_map/ppermute | solution.py:458
  230.7 12.1 %collective-permute-done.38 = bf16[512,1024]{1,0:T(8,128)(2,1)S(1)} collective-permute-done((bf16[512,1024]{1,0:T(8,128)(2,1)S(1)}, bf16[512,1024]{1,0:T(8,128)(2,1)S(1)}, u32[]{:S(2)}, u32[]{:S(2)}) %collective-permute-start.38) | collective-permute-done | bytes 1048608 | tf_op jit(solution)/shard_map/ppermute | solution.py:454
  244.0 21.1 %collective-permute-done.39 = bf16[1024,512]{1,0:T(8,128)(2,1)S(1)} collective-permute-done((bf16[1024,512]{1,0:T(8,128)(2,1)S(1)}, bf16[1024,512]{1,0:T(8,128)(2,1)S(1)}, u32[]{:S(2)}, u32[]{:S(2)}) %collective-permute-start.39) | collective-permute-done | bytes 1048608 | tf_op jit(solution)/shard_map/ppermute | solution.py:454
  268.7 4.5 fusion.165
  273.2 4.6 fusion.163
  277.9 4.5 fusion.161
  282.5 11.9 %multiply_reduce_fusion.12 = (f32[544]{0:T(1024)S(1)}, f32[544]{0:T(1024)S(1)}, f32[544,2048]{1,0:T(8,128)S(1)}) fusion(f32[2048]{0:T(1024)S(1)} %copy-done.75, f32[544,2048]{1,0:T(8,128)S(1)} %bitcast.129, f32[544]{0:T(1024)S(1)} %fusion.119, f32[2048]{0:T(1024)S(1)} %bitcast.182, f32[540,2048]{1,0:T(8,128)} %get-tuple-element.69, ...), kind=kLoop, calls=%fused_computation.60 | loop fusion | flops 33422272 | bytes 49109376 | tf_op jit(solution)/shard_map/reduce_sum | solution.py:674
  317.0 6.3 %collective-permute-done.30 = bf16[512,256]{1,0:T(8,128)(2,1)S(1)} collective-permute-done((bf16[512,256]{1,0:T(8,128)(2,1)S(1)}, bf16[512,256]{1,0:T(8,128)(2,1)S(1)}, u32[]{:S(2)}, u32[]{:S(2)}) %collective-permute-start.30) | collective-permute-done | bytes 262176 | tf_op jit(solution)/shard_map/ppermute | solution.py:454
  331.8 5.5 %collective-permute-done.32 = bf16[3,512,128]{2,1,0:T(8,128)(2,1)S(1)} collective-permute-done((bf16[3,512,128]{2,1,0:T(8,128)(2,1)S(1)}, bf16[3,512,128]{2,1,0:T(8,128)(2,1)S(1)}, u32[]{:S(2)}, u32[]{:S(2)}) %collective-permute-start.32) | collective-permute-done | bytes 393248 | tf_op jit(solution)/shard_map/ppermute | solution.py:454
  342.5 16.4 %collective-permute-done.31 = bf16[512,1024]{1,0:T(8,128)(2,1)S(1)} collective-permute-done((bf16[512,1024]{1,0:T(8,128)(2,1)S(1)}, bf16[512,1024]{1,0:T(8,128)(2,1)S(1)}, u32[]{:S(2)}, u32[]{:S(2)}) %collective-permute-start.31) | collective-permute-done | bytes 1048608 | tf_op jit(solution)/shard_map/ppermute | solution.py:454
  362.6 17.7 %multiply_reduce_fusion.3 = (f32[2048]{0:T(1024)S(1)}, f32[2048]{0:T(1024)S(1)}, f32[2048]{0:T(1024)S(1)}, f32[2048]{0:T(1024)S(1)}, f32[2048]{0:T(1024)S(1)}, /...) fusion(f32[544,2048]{1,0:T(8,128)} %copy-done, f32[544,2048]{1,0:T(8,128)} %copy-done.1), kind=kLoop, calls=%fused_computation.46 | loop fusion | flops 18855936 | bytes 42016768 | tf_op jit(solution)/shard_map/reduce_sum | solution.py:665
  382.6 40.4 %all-reduce.1 = (f32[512]{0:T(512)}, f32[512]{0:T(512)}, f32[512]{0:T(512)}, f32[512]{0:T(512)}) all-reduce(f32[512]{0:T(512)S(1)} %get-tuple-element.30, f32[512]{0:T(512)S(1)} %get-tuple-element.28, f32[512]{0:T(512)S(1)} %copy-done.113, f32[512]{0:T(512)S(1)} %copy-done.115), channel_id=1, replica_groups=mesh['dp'=16,'mp'=2] {'dp','mp'}, use_global_device_ids=true, to_apply=%region_24.25 | all-reduce | flops 2048 | bytes 16384 | tf_op jit(solution)/shard_map/psum | solution.py:705
  423.0 61.1 %all-reduce.2 = (bf16[1024]{0:T(1024)(128)(2,1)S(1)}, bf16[9,1024]{1,0:T(8,128)(2,1)S(1)}) all-reduce(bf16[1024]{0:T(1024)(128)(2,1)S(1)} %fusion.115, bf16[9,1024]{1,0:T(8,128)(2,1)S(1)} %fusion.113), channel_id=1, replica_groups=mesh['dp'=16,'mp'=2] {'dp'}, use_global_device_ids=true, to_apply=%region_32.33 | all-reduce | flops 10240 | bytes 40960 | tf_op jit(solution)/shard_map/psum | solution.py:715
  486.1 9.7 %all-reduce.6.cloned.1.call-done = (bf16[512,256]{1,0:T(8,128)(2,1)}, bf16[512,256]{1,0:T(8,128)(2,1)}, bf16[512,1024]{1,0:T(8,128)(2,1)}, bf16[3,512,128]{2,1,0...) async-done(((bf16[512,256]{1,0:T(8,128)(2,1)}, ...) | async-done | bytes 5636112 | tf_op jit(solution)/shard_map/psum | solution.py:715
  (489 shorter events, 186.9 us)
Async XLA Ops:
  7.2 488.6 %all-reduce.6.cloned.1.call-start = ((), (), s32[]{:S(2)}) async-start(), calls=%async_computation | async-start | bytes 11272192 | tf_op jit(solution)/shard_map/psum | solution.py:715
  7.3 20.3 %collective-permute-start.6 = (s32[1]{0:T(128)}, s32[1]{0:T(128)}, u32[]{:S(2)}, u32[]{:S(2)}) collective-permute-start(s32[1]{0:T(128)} %param.19), channel_id=1, source_target_pairs={{1,2},{2,1},{5,6},{6,5},{9,10},{10,9},{13,14},{14,13},{17,18},{18,... | collective-permute-start | bytes 20 | tf_op jit(solution)/shard_map/ppermute | solution.py:474
  8.6 21.5 %collective-permute-start.11 = (bf16[1024]{0:T(1024)(128)(2,1)}, bf16[1024]{0:T(1024)(128)(2,1)S(1)}, u32[]{:S(2)}, u32[]{:S(2)}) collective-permute-start(bf16[1024]{0:T(1024)(128)(2,1)} %param.26), channel_id=1, source_target_pairs={{0,1},{1,0},{2,3},{3,2},{4,5},{5,4},{6,7},{7,6},{8,9},{9,8},{10,11... | collective-permute-start | bytes 6152 | tf_op jit(solution)/shard_map/ppermute | solution.py:454
  13.7 16.6 %collective-permute-start = (bf16[16,512]{1,0:T(8,128)(2,1)}, bf16[16,512]{1,0:T(8,128)(2,1)}, u32[]{:S(2)}, u32[]{:S(2)}) collective-permute-start(bf16[16,512]{1,0:T(8,128)(2,1)} %select_bitcast_fusion.2), channel_id=1, source_target_pairs={{0,2},{1,0},{2,3},{3,1},{4,6},{5,4},{6,7},{7,5},{8,10},{9,8},{10,1... | collective-permute-start | bytes 49160 | tf_op jit(solution)/shard_map/ppermute | solution.py:482
  13.8 19.2 %collective-permute-start.12 = (bf16[9,1024]{1,0:T(8,128)(2,1)}, bf16[9,1024]{1,0:T(8,128)(2,1)}, u32[]{:S(2)}, u32[]{:S(2)}) collective-permute-start(bf16[9,1024]{1,0:T(8,128)(2,1)} %param.27), channel_id=1, source_target_pairs={{0,1},{1,0},{2,3},{3,2},{4,5},{5,4},{6,7},{7,6},{8,9},{9,8},{10,11... | collective-permute-start | bytes 55304 | tf_op jit(solution)/shard_map/ppermute | solution.py:454
  30.1 79.1 %collective-permute-start.18 = (bf16[128,512]{1,0:T(8,128)(2,1)}, bf16[128,512]{1,0:T(8,128)(2,1)}, u32[]{:S(2)}, u32[]{:S(2)}) collective-permute-start(bf16[128,512]{1,0:T(8,128)(2,1)} %constant_dynamic-slice_fusion.2), channel_id=1, source_target_pairs={{0,1},{1,0},{2,3},{3,2},{4,5},{5,4},{6,7},{7,6},{8,9},{9,8},{10,11... | collective-permute-start | bytes 393224 | tf_op jit(solution)/shard_map/ppermute | solution.py:454
  33.0 30.6 %collective-permute-start.1 = (bf16[512,512]{1,0:T(8,128)(2,1)S(1)}, bf16[512,512]{1,0:T(8,128)(2,1)S(1)}, u32[]{:S(2)}, u32[]{:S(2)}) collective-permute-start(bf16[512,512]{1,0:T(8,128)(2,1)S(1)} %bitcast.164), channel_id=1, source_target_pairs={{1,2},{2,1},{5,6},{6,5},{9,10},{10,9},{13,14},{14,13},{17,18},{18,... | collective-permute-start | bytes 1572872 | tf_op jit(solution)/shard_map/ppermute | solution.py:474
  41.1 22.6 %collective-permute-start.15 = (bf16[768,256]{1,0:T(8,128)(2,1)S(1)}, bf16[768,256]{1,0:T(8,128)(2,1)S(1)}, u32[]{:S(2)}, u32[]{:S(2)}) collective-permute-start(bf16[768,256]{1,0:T(8,128)(2,1)S(1)} %constant_dynamic-slice_fusion.3), channel_id=1, source_target_pairs={{0,1},{1,0},{2,3},{3,2},{4,5},{5,4},{6,7},{7,6},{8,9},{9,8},{10,11... | collective-permute-start | bytes 1179656 | tf_op jit(solution)/shard_map/ppermute | solution.py:454
  43.7 20.0 %collective-permute-start.13 = (bf16[512,256]{1,0:T(8,128)(2,1)S(1)}, bf16[512,256]{1,0:T(8,128)(2,1)S(1)}, u32[]{:S(2)}, u32[]{:S(2)}) collective-permute-start(bf16[512,256]{1,0:T(8,128)(2,1)S(1)} %constant_dynamic-slice_fusion.4), channel_id=1, source_target_pairs={{0,1},{1,0},{2,3},{3,2},{4,5},{5,4},{6,7},{7,6},{8,9},{9,8},{10,11... | collective-permute-start | bytes 786440 | tf_op jit(solution)/shard_map/ppermute | solution.py:454
  44.4 42.3 %collective-permute-start.22 = (bf16[512,512]{1,0:T(8,128)(2,1)S(1)}, bf16[512,512]{1,0:T(8,128)(2,1)}, u32[]{:S(2)}, u32[]{:S(2)}) collective-permute-start(bf16[512,512]{1,0:T(8,128)(2,1)S(1)} %constant_dynamic-slice_fusion), channel_id=1, source_target_pairs={{0,1},{1,0},{2,3},{3,2},{4,5},{5,4},{6,7},{7,6},{8,9},{9,8},{10,11... | collective-permute-start | bytes 1572872 | tf_op jit(solution)/shard_map/ppermute | solution.py:454
  63.7 22.5 %collective-permute-start.7 = (bf16[256,1024]{1,0:T(8,128)(2,1)S(1)}, bf16[256,1024]{1,0:T(8,128)(2,1)S(1)}, u32[]{:S(2)}, u32[]{:S(2)}) collective-permute-start(bf16[256,1024]{1,0:T(8,128)(2,1)S(1)} %constant_dynamic-slice_fusion.6), channel_id=1, source_target_pairs={{0,1},{1,0},{2,3},{3,2},{4,5},{5,4},{6,7},{7,6},{8,9},{9,8},{10,11... | collective-permute-start | bytes 1572872 | tf_op jit(solution)/shard_map/ppermute | solution.py:454
  63.7 24.7 %collective-permute-start.16 = (bf16[768,256]{1,0:T(8,128)(2,1)S(1)}, bf16[768,256]{1,0:T(8,128)(2,1)S(1)}, u32[]{:S(2)}, u32[]{:S(2)}) collective-permute-start(bf16[768,256]{1,0:T(8,128)(2,1)S(1)} %collective-permute-done.15), channel_id=1, source_target_pairs={{0,2},{2,0},{4,6},{6,4},{8,10},{10,8},{12,14},{14,12},{16,18},{18,... | collective-permute-start | bytes 1179656 | tf_op jit(solution)/shard_map/ppermute | solution.py:458
  71.2 38.5 %collective-permute-start.20 = (bf16[256,1024]{1,0:T(8,128)(2,1)}, bf16[256,1024]{1,0:T(8,128)(2,1)}, u32[]{:S(2)}, u32[]{:S(2)}) collective-permute-start(bf16[256,1024]{1,0:T(8,128)(2,1)} %constant_dynamic-slice_fusion.1), channel_id=1, source_target_pairs={{0,1},{1,0},{2,3},{3,2},{4,5},{5,4},{6,7},{7,6},{8,9},{9,8},{10,11... | collective-permute-start | bytes 1572872 | tf_op jit(solution)/shard_map/ppermute | solution.py:454
  86.7 27.5 %collective-permute-start.25 = (bf16[512,512]{1,0:T(8,128)(2,1)}, bf16[512,512]{1,0:T(8,128)(2,1)}, u32[]{:S(2)}, u32[]{:S(2)}) collective-permute-start(bf16[512,512]{1,0:T(8,128)(2,1)} %bitcast.29), channel_id=1, source_target_pairs={{1,2},{2,1},{5,6},{6,5},{9,10},{10,9},{13,14},{14,13},{17,18},{18,... | collective-permute-start | bytes 1572872 | tf_op jit(solution)/shard_map/ppermute | solution.py:474
  88.4 27.1 %collective-permute-start.23 = (bf16[512,512]{1,0:T(8,128)(2,1)}, bf16[512,512]{1,0:T(8,128)(2,1)}, u32[]{:S(2)}, u32[]{:S(2)}) collective-permute-start(bf16[512,512]{1,0:T(8,128)(2,1)} %collective-permute-done.22), channel_id=1, source_target_pairs={{0,2},{2,0},{4,6},{6,4},{8,10},{10,8},{12,14},{14,12},{16,18},{18,... | collective-permute-start | bytes 1572872 | tf_op jit(solution)/shard_map/ppermute | solution.py:458
  203.2 39.5 %collective-permute-start.38 = (bf16[512,1024]{1,0:T(8,128)(2,1)S(1)}, bf16[512,1024]{1,0:T(8,128)(2,1)S(1)}, u32[]{:S(2)}, u32[]{:S(2)}) collective-permute-start(bf16[512,1024]{1,0:T(8,128)(2,1)S(1)} %dynamic_slice.231), channel_id=1, source_target_pairs={{0,1},{1,0},{2,3},{3,2},{4,5},{5,4},{6,7},{7,6},{8,9},{9,8},{10,11... | collective-permute-start | bytes 3145736 | tf_op jit(solution)/shard_map/ppermute | solution.py:454
  205.9 59.2 %collective-permute-start.39 = (bf16[1024,512]{1,0:T(8,128)(2,1)S(1)}, bf16[1024,512]{1,0:T(8,128)(2,1)S(1)}, u32[]{:S(2)}, u32[]{:S(2)}) collective-permute-start(bf16[1024,512]{1,0:T(8,128)(2,1)S(1)} %dynamic_slice.230), channel_id=1, source_target_pairs={{0,1},{1,0},{2,3},{3,2},{4,5},{5,4},{6,7},{7,6},{8,9},{9,8},{10,11... | collective-permute-start | bytes 3145736 | tf_op jit(solution)/shard_map/ppermute | solution.py:454
  215.0 51.5 %collective-permute-start.27 = (bf16[16,256]{1,0:T(8,128)(2,1)S(1)}, bf16[16,256]{1,0:T(8,128)(2,1)S(1)}, u32[]{:S(2)}, u32[]{:S(2)}) collective-permute-start(bf16[16,256]{1,0:T(8,128)(2,1)S(1)} %slice_select_fusion), channel_id=1, source_target_pairs={{0,2},{2,0},{4,6},{6,4},{8,10},{10,8},{12,14},{14,12},{16,18},{18,... | collective-permute-start | bytes 24584 | tf_op jit(solution)/shard_map/ppermute | solution.py:458
  226.2 112.0 %collective-permute-start.35 = (bf16[1024,256]{1,0:T(8,128)(2,1)}, bf16[1024,256]{1,0:T(8,128)(2,1)}, u32[]{:S(2)}, u32[]{:S(2)}) collective-permute-start(bf16[1024,256]{1,0:T(8,128)(2,1)} %dynamic_slice.234), channel_id=1, source_target_pairs={{0,1},{1,0},{2,3},{3,2},{4,5},{5,4},{6,7},{7,6},{8,9},{9,8},{10,11... | collective-permute-start | bytes 1572872 | tf_op jit(solution)/shard_map/ppermute | solution.py:454
  228.9 111.3 %collective-permute-start.36 = (bf16[3,512,256]{2,1,0:T(8,128)(2,1)}, bf16[3,512,256]{2,1,0:T(8,128)(2,1)}, u32[]{:S(2)}, u32[]{:S(2)}) collective-permute-start(bf16[3,512,256]{2,1,0:T(8,128)(2,1)} %dynamic_slice.233), channel_id=1, source_target_pairs={{0,1},{1,0},{2,3},{3,2},{4,5},{5,4},{6,7},{7,6},{8,9},{9,8},{10,11... | collective-permute-start | bytes 2359304 | tf_op jit(solution)/shard_map/ppermute | solution.py:454
  311.8 111.1 %collective-permute-start.33 = (bf16[1024]{0:T(1024)(128)(2,1)S(1)}, bf16[1024]{0:T(1024)(128)(2,1)S(1)}, u32[]{:S(2)}, u32[]{:S(2)}) collective-permute-start(bf16[1024]{0:T(1024)(128)(2,1)S(1)} %dynamic_slice.238), channel_id=1, source_target_pairs={{0,1},{1,0},{2,3},{3,2},{4,5},{5,4},{6,7},{7,6},{8,9},{9,8},{10,11... | collective-permute-start | bytes 6152 | tf_op jit(solution)/shard_map/ppermute | solution.py:454
  328.9 30.0 %collective-permute-start.31 = (bf16[512,1024]{1,0:T(8,128)(2,1)S(1)}, bf16[512,1024]{1,0:T(8,128)(2,1)S(1)}, u32[]{:S(2)}, u32[]{:S(2)}) collective-permute-start(bf16[512,1024]{1,0:T(8,128)(2,1)S(1)} %dynamic_slice.232), channel_id=1, source_target_pairs={{0,1},{1,0},{2,3},{3,2},{4,5},{5,4},{6,7},{7,6},{8,9},{9,8},{10,11... | collective-permute-start | bytes 3145736 | tf_op jit(solution)/shard_map/ppermute | solution.py:454
  361.9 123.4 %collective-permute-start.28 = (bf16[512,512]{1,0:T(8,128)(2,1)S(1)}, bf16[512,512]{1,0:T(8,128)(2,1)S(1)}, u32[]{:S(2)}, u32[]{:S(2)}) collective-permute-start(bf16[512,512]{1,0:T(8,128)(2,1)S(1)} %add_convert_fusion.1), channel_id=1, source_target_pairs={{1,2},{2,1},{5,6},{6,5},{9,10},{10,9},{13,14},{14,13},{17,18},{18,... | collective-permute-start | bytes 1572872 | tf_op jit(solution)/shard_map/ppermute | solution.py:474
  380.5 42.5 %collective-permute-start.34 = (bf16[9,1024]{1,0:T(8,128)(2,1)S(1)}, bf16[9,1024]{1,0:T(8,128)(2,1)S(1)}, u32[]{:S(2)}, u32[]{:S(2)}) collective-permute-start(bf16[9,1024]{1,0:T(8,128)(2,1)S(1)} %dynamic_slice.237), channel_id=1, source_target_pairs={{0,1},{1,0},{2,3},{3,2},{4,5},{5,4},{6,7},{7,6},{8,9},{9,8},{10,11... | collective-permute-start | bytes 55304 | tf_op jit(solution)/shard_map/ppermute | solution.py:454
  (141 other events, 1779.0 us)
Sparse Core Ops, SparseCore 0:
  360.4 135.3 all-reduce.5

commit v2 on v0

--- a/solution.py
+++ b/solution.py
@@ -1,12 +1,16 @@
+import functools
 import math
 
 import jax
 import jax.numpy as jnp
 from jax import lax
+from jax.experimental import pallas as pl
+from jax.experimental.pallas import tpu as pltpu
 from jax.sharding import PartitionSpec as P
 
 FF = 2048
 HEAD_DIM = 64
+EDGE = 16
 
 
 epsilon = 1e-06
@@ -445,6 +449,1479 @@
     )
 
 
+HALF = 256
+LANES = 128
+
+
+def dot_nn(left_side, right_side):
+    return lax.dot_general(
+        left_side, right_side, (((1,), (0,)), ((), ())), preferred_element_type=jnp.float32
+    )
+
+
+def dot_nt(left_side, right_side):
+    return lax.dot_general(
+        left_side, right_side, (((1,), (1,)), ((), ())), preferred_element_type=jnp.float32
+    )
+
+
+def dot_tn(left_side, right_side):
+    return lax.dot_general(
+        left_side, right_side, (((0,), (0,)), ((), ())), preferred_element_type=jnp.float32
+    )
+
+
+def row_stats(values):
+    centre = values - jnp.mean(values, axis=-1, keepdims=True)
+    inv = lax.rsqrt(jnp.mean(centre * centre, axis=-1, keepdims=True) + epsilon)
+    return centre * inv, inv
+
+
+def norm_grad(grad_out, unit, inv, gain):
+    scaled = grad_out * gain
+    mean_one = jnp.mean(scaled, axis=-1, keepdims=True)
+    mean_two = jnp.mean(scaled * unit, axis=-1, keepdims=True)
+    return inv * (scaled - mean_one - unit * mean_two)
+
+
+def sigmoid(values):
+    return 0.5 * jnp.tanh(0.5 * values) + 0.5
+
+
+def silu(values):
+    return values * sigmoid(values)
+
+
+def turned(values):
+    return jnp.transpose(values.astype(jnp.float32)).astype(jnp.bfloat16)
+
+
+class Loader:
+    def __init__(self, sems):
+        self.sems = sems
+        self.count = 0
+        self.waits = []
+
+    def start(self, source, target):
+        copy = pltpu.make_async_copy(source, target, self.sems.at[self.count])
+        self.count += 1
+        copy.start()
+        self.waits.append(copy)
+
+    def either(self, first, second, use_first, target):
+        sem = self.sems.at[self.count]
+        self.count += 1
+
+        @pl.when(use_first)
+        def _():
+            pltpu.make_async_copy(first, target, sem).start()
+
+        @pl.when(jnp.logical_not(use_first))
+        def _():
+            pltpu.make_async_copy(second, target, sem).start()
+
+        self.waits.append(pltpu.make_async_copy(first, target, sem))
+
+    def wait(self):
+        for copy in self.waits:
+            copy.wait()
+        self.waits = []
+
+
+def load_pair(loader, own, got, part, taker, core, target, slots=(0, 1)):
+    loader.start(own, target.at[slots[0]])
+    loader.either(got, part, core == taker, target.at[slots[1]])
+
+
+def load_left(loader, w_left, got, part, core, target):
+    blocks = w_left.shape[1] // HALF
+    rows = w_left.shape[0]
+    for block in range(blocks):
+        loader.start(w_left.at[:, pl.ds(block * HALF, HALF)], target.at[block])
+        at = pl.ds(block * rows, rows)
+        loader.either(got.at[at], part.at[at], core == 0, target.at[blocks + block])
+
+
+def load_pack(loader, got, part, core, target):
+    count, depth = target.shape[:2]
+    for block in range(count):
+        at = pl.ds(got.shape[0] - (count - block) * depth, depth)
+        loader.either(got.at[at], part.at[at], core == 0, target.at[block])
+
+
+def load_point(loader, w_point, got, part, core, target):
+    at = pl.ds(0, w_point.shape[0])
+    load_pair(loader, w_point, got.at[at], part.at[at], 1, core, target)
+
+
+def load_right(loader, w_right, got, part, core, target):
+    loader.start(w_right, target.at[0])
+    rows = w_right.shape[1]
+    for tap in range(w_right.shape[0]):
+        at = (pl.ds(2 * rows + (tap // 2) * rows, rows), pl.ds((tap % 2) * LANES, LANES))
+        loader.either(got.at[at], part.at[at], core == 1, target.at[1, tap])
+
+
+def load_qkv(loader, w_qkv, got, part, core, target, which):
+    rows = w_qkv.shape[1]
+    for slot, index in enumerate(which):
+        loader.start(w_qkv.at[index], target.at[0, slot])
+        at = pl.ds(index * rows, rows)
+        loader.either(got.at[at], part.at[at], core == 0, target.at[1, slot])
+
+
+def load_out(loader, w_out, got, part, core, target):
+    loader.start(w_out, target.at[0])
+    rows = w_out.shape[0]
+    for block in range(2):
+        at = pl.ds(block * rows, rows)
+        loader.either(
+            got.at[at], part.at[at], core == 1, target.at[1, :, pl.ds(block * HALF, HALF)]
+        )
+
+
+def load_in(loader, w_in, got2, part2, got3, part3, core, target):
+    blocks = w_in.shape[1] // HALF
+    rows = w_in.shape[0]
+    for block in range(blocks):
+        loader.start(w_in.at[:, pl.ds(block * HALF, HALF)], target.at[block])
+        got, part = (got2, part2) if block < 2 else (got3, part3)
+        at = pl.ds(rows + (block % 2) * rows, rows)
+        loader.either(got.at[at], part.at[at], core == 1, target.at[blocks + block])
+
+
+def load_back(loader, w_back, got, part, core, target):
+    loader.start(w_back, target.at[0])
+    rows = w_back.shape[0]
+    half = rows // 2
+    near, far = pl.ds(0, HALF), pl.ds(HALF, HALF)
+    for at, taker, spot in (
+        (pl.ds(0, rows), 0, (pl.ds(0, rows), near)),
+        (pl.ds(rows, half), 0, (pl.ds(0, half), far)),
+        (pl.ds(0, half), 1, (pl.ds(half, half), far)),
+    ):
+        loader.either(got.at[at], part.at[at], core == taker, target.at[1].at[spot])
+
+
+GROUP = 8
+
+
+def row_spot(rows, own, lanes):
+    row = lax.broadcasted_iota(jnp.int32, (rows, lanes), 0)
+    spot = (row % GROUP) * (own // GROUP) + row // GROUP
+    return jnp.where(row < own, spot, jnp.where(row < own + EDGE, row - own - EDGE, row - EDGE))
+
+
+def row_mask(core, length, ext, lanes):
+    own = ext - 2 * EDGE
+    spot = row_spot(ext, own, lanes) + core * own
+    return jnp.where((spot >= 0) & (spot < length), 1.0, 0.0)
+
+
+def lane_tiles(width):
+    return [slice(at, at + LANES) for at in range(0, width, LANES)]
+
+
+def load_tiles(source, tiles):
+    for index, lanes in enumerate(lane_tiles(source.shape[1])):
+        tiles[index] = source[:, lanes].astype(jnp.float32)
+
+
+def gather_rows(tiles, target):
+    own = tiles.shape[1]
+    for tile, lanes in enumerate(lane_tiles(target.shape[1])):
+        for index in range(own // GROUP):
+            target[index * GROUP : (index + 1) * GROUP, lanes] = tiles[
+                tile, pl.ds(index, GROUP, stride=own // GROUP)
+            ]
+
+
+def scatter_rows(source, tiles, target):
+    own = tiles.shape[1]
+    for tile, lanes in enumerate(lane_tiles(target.shape[1])):
+        for index in range(own // GROUP):
+            tiles[tile, pl.ds(index, GROUP, stride=own // GROUP)] = source[
+                index * GROUP : (index + 1) * GROUP, lanes
+            ]
+        target[:, lanes] = tiles[tile].astype(target.dtype)
+
+
+def next_group(first, row):
+    sub = lax.broadcasted_iota(jnp.int32, first.shape, 0)
+    return jnp.where(sub == GROUP - 1, row, pltpu.roll(first, GROUP - 1, 0))
+
+
+def previous_group(last, row):
+    sub = lax.broadcasted_iota(jnp.int32, last.shape, 0)
+    return jnp.where(sub == 0, row, pltpu.roll(last, 1, 0))
+
+
+def shift_rows(values, offset):
+    if offset == 0:
+        return values
+    ext = values.shape[0]
+    own = ext - 2 * EDGE
+    mid, before, after = values[:own], values[own : own + EDGE], values[own + EDGE :]
+    sub = lax.broadcasted_iota(jnp.int32, before.shape, 0)
+    if offset > 0:
+        moved = jnp.concatenate([mid[GROUP:], next_group(mid[:GROUP], after[:1])], axis=0)
+        before = jnp.where(sub == EDGE - 1, mid[:1], pltpu.roll(before, EDGE - 1, 0))
+        after = pltpu.roll(after, EDGE - 1, 0)
+    else:
+        moved = jnp.concatenate(
+            [previous_group(mid[own - GROUP :], before[EDGE - 1 :]), mid[: own - GROUP]], axis=0
+        )
+        after = jnp.where(sub == 0, mid[own - 1 :], pltpu.roll(after, 1, 0))
+        before = pltpu.roll(before, 1, 0)
+    return jnp.concatenate([moved, before, after], axis=0)
+
+
+def fill_window(window, values, own, reach):
+    before, after = values[own : own + EDGE], values[own + EDGE :]
+    window[reach * GROUP : reach * GROUP + own] = values[:own]
+    for step in range(1, reach + 1):
+        last = values[own - step * GROUP : own - (step - 1) * GROUP]
+        at = (reach - step) * GROUP
+        window[at : at + GROUP] = previous_group(last, before[EDGE - step : EDGE - step + 1])
+        first = values[(step - 1) * GROUP : step * GROUP]
+        at = reach * GROUP + own + (step - 1) * GROUP
+        window[at : at + GROUP] = next_group(first, after[step - 1 : step])
+
+
+def glu_kernel(
+    info, block, moved, edge, gain_glu, gain_branch, w_value, w_gate, got, part_w,
+    resid_o, branch_o, gluin_o, value_o, sig_o, x_s, n_s, wv_s, wg_s, sems,
+):
+    core, member, length = info[0], info[1], info[2]
+    loader = Loader(sems)
+    load_pair(loader, w_value, got, part_w, 0, core, wv_s, (member, 1 - member))
+    load_pair(loader, w_gate, got, part_w, 1, core, wg_s, (member, 1 - member))
+    ext = x_s.shape[0]
+    rows = ext - 2 * EDGE
+    edge_f = edge[...].astype(jnp.float32)
+    x_s[rows : rows + EDGE] = jnp.where(core == 1, edge_f, 0.0)
+    x_s[rows + EDGE :] = jnp.where(core == 1, 0.0, edge_f)
+
+    @pl.when(core == member)
+    def _():
+        load_tiles(block, n_s)
+
+    @pl.when(core != member)
+    def _():
+        load_tiles(moved, n_s)
+
+    gather_rows(n_s, x_s)
+    loader.wait()
+    valid = row_mask(core, length, ext, LANES)[:, :1]
+    part = ext // 2
+    for start in (0, part):
+        at = slice(start, start + part)
+        x = x_s[at]
+        glu_in = (row_stats(x)[0] * gain_glu[...]).astype(jnp.bfloat16)
+        gluin_o[at] = glu_in
+        for half in range(2):
+            cols = slice(half * HALF, (half + 1) * HALF)
+            value = dot_nn(glu_in, wv_s[half])
+            sig = sigmoid(dot_nn(glu_in, wg_s[half]))
+            value_o[at, cols] = value.astype(jnp.bfloat16)
+            sig_o[at, cols] = sig.astype(jnp.bfloat16)
+            resid_o[at, cols] = x[:, cols] + (value * sig).astype(jnp.bfloat16).astype(jnp.float32)
+        normed = row_stats(resid_o[at])[0] * gain_branch[...]
+        branch_o[at] = (valid[at] * normed).astype(jnp.bfloat16)
+
+
+def spread_block(index, size, stride):
+    source = lax.broadcasted_iota(jnp.int32, (size, size), 0)
+    channel = lax.broadcasted_iota(jnp.int32, (size, size), 1) + index * size
+    return jnp.where(channel == source * stride, 1.0, 0.0).astype(jnp.bfloat16)
+
+
+def fill_taps(pack_own, pack_oth, taps_s):
+    count, cols = pack_own.shape
+    taps_s[:count, :cols] = pack_own[...].astype(jnp.float32)
+    for block in range(pack_oth.shape[0]):
+        at = cols + block * HALF
+        taps_s[:, at : at + HALF] = pack_oth[block].astype(jnp.float32)
+
+
+def branch_kernel(
+    info, branch, resid_one, pack_own, w_left, w_right, w_point, got, part,
+    resid_two_o, left_o, right_o, stats_o, depth_o,
+    wl_s, wr_s, wp_s, po_s, taps_s, mid_s, din_s, sums_s, sep_s, sems,
+):
+    core, length = info[0], info[2]
+    loader = Loader(sems)
+    load_right(loader, w_right, got, part, core, wr_s)
+    load_left(loader, w_left, got, part, core, wl_s)
+    load_point(loader, w_point, got, part, core, wp_s)
+    load_pack(loader, got, part, core, po_s)
+    ext = branch.shape[0]
+    rows = ext - 2 * EDGE
+    chunks = wl_s.shape[0]
+    per_shard = chunks // 2
+    conv_taps = wr_s.shape[1]
+    sep_taps = pack_own.shape[0] - 1
+    inner = chunks * HALF
+    stride = inner // (2 * wr_s.shape[3])
+    loader.wait()
+    fill_taps(pack_own, po_s, taps_s)
+    right_pre = jnp.zeros((ext, 2 * wr_s.shape[3]), jnp.float32)
+    for tap in range(conv_taps):
+        product = jnp.concatenate(
+            [dot_nn(branch[...], wr_s[0, tap]), dot_nn(branch[...], wr_s[1, tap])], axis=1
+        )
+        right_pre = right_pre + shift_rows(product, tap - conv_taps // 2)
+    right_o[...] = right_pre
+    right_act = silu(right_pre).astype(jnp.bfloat16)
+    sums_s[...] = jnp.zeros_like(sums_s)
+
+    def first(index, carry):
+        left_pre = dot_nn(branch[...], wl_s[index])
+        left_o[index] = left_pre.astype(jnp.bfloat16)
+        mid = silu(left_pre) + dot_nn(right_act, spread_block(index, HALF, stride))
+        mid_s[index] = mid
+        near, far = mid[:, :LANES], mid[:, LANES:]
+        sums_s[0] += near + far
+        sums_s[1] += near * near + far * far
+        return carry
+
+    lax.fori_loop(0, chunks, first, 0)
+    mean = jnp.sum(sums_s[0], axis=-1, keepdims=True) / inner
+    inv = lax.rsqrt(
+        jnp.sum(sums_s[1], axis=-1, keepdims=True) / inner - mean * mean + epsilon
+    )
+    lane = lax.broadcasted_iota(jnp.int32, (ext, LANES), 1)
+    stats_o[...] = jnp.where(lane == 0, mean, inv)
+    sums_s[0] = jnp.broadcast_to(mean, (ext, LANES))
+    sums_s[1] = inv * row_mask(core, length, ext, LANES)
+    sep_s[...] = jnp.zeros_like(sep_s)
+
+    def second(index, carry):
+        cols = pl.ds(pl.multiple_of(index * HALF, HALF), HALF)
+        taps = taps_s[:, cols]
+        for side in range(2):
+            lanes = slice(side * LANES, (side + 1) * LANES)
+            depth_in = (
+                (mid_s[index, :, lanes] - sums_s[0]) * sums_s[1] * taps[sep_taps : sep_taps + 1, lanes]
+            )
+            fill_window(din_s.at[:, lanes], depth_in, rows, sep_taps // 2)
+        step = 64
+        for start in range(0, rows, step):
+            for side in range(2):
+                lanes = slice(side * LANES, (side + 1) * LANES)
+                acc = din_s[start : start + step, lanes] * taps[:1, lanes]
+                for tap in range(1, sep_taps):
+                    at = start + tap * GROUP
+                    acc = acc + din_s[at : at + step, lanes] * taps[tap : tap + 1, lanes]
+                depth_o[index, start : start + step, lanes] = acc.astype(jnp.bfloat16)
+        shard, chunk = index // per_shard, index % per_shard
+        point = wp_s[shard, pl.ds(pl.multiple_of(chunk * HALF, HALF), HALF)]
+        sep_s[...] += dot_nn(depth_o[index], point)
+        return carry
+
+    lax.fori_loop(0, chunks, second, 0)
+    sep_width = sep_s.shape[1]
+    resid_two_o[:, :sep_width] = resid_one[:rows, :sep_width] + sep_s[...]
+    resid_two_o[:, sep_width:] = resid_one[:rows, sep_width:]
+
+
+def kv_kernel(info, resid_two, gain, w_qkv, got, part, attn_o, kv_o, w_s, sems):
+    loader = Loader(sems)
+    load_qkv(loader, w_qkv, got, part, info[0], w_s, (1, 2))
+    attn_in = (row_stats(resid_two[...])[0] * gain[...]).astype(jnp.bfloat16)
+    attn_o[...] = attn_in
+    loader.wait()
+    width = w_s.shape[3]
+    for shard in range(2):
+        for index in range(2):
+            at = (2 * index + shard) * width
+            kv_o[:, at : at + width] = dot_nn(attn_in, w_s[shard, index]).astype(jnp.bfloat16)
+
+
+def query_kernel(info, attn_in, w_qkv, got, part, q_o, w_s, sems):
+    loader = Loader(sems)
+    load_qkv(loader, w_qkv, got, part, info[0], w_s, (0,))
+    loader.wait()
+    width = w_s.shape[3]
+    scale = 1.0 / math.sqrt(HEAD_DIM)
+    for shard in range(2):
+        query = dot_nn(attn_in[...], w_s[shard, 0]).astype(jnp.bfloat16).astype(jnp.float32)
+        q_o[:, shard * width : (shard + 1) * width] = (query * scale).astype(jnp.bfloat16)
+
+
+def key_bias(core, length, rows):
+    row = lax.broadcasted_iota(jnp.int32, (2 * rows, LANES), 0)
+    far = jnp.where(row < rows, 0, 1)
+    spot = (row % GROUP) * (rows // GROUP) + (row - far * rows) // GROUP
+    spot = spot + jnp.where(core == far, 0, 1) * rows
+    return jnp.where(spot < length, 0.0, negative_big)
+
+
+def head_masks(rows, head):
+    lane = lax.broadcasted_iota(jnp.int32, (rows, LANES), 1)
+    return (lane // HEAD_DIM) == head, lane == HEAD_DIM * (1 - head)
+
+
+def attend_kernel(info, q, kvo, kvf, ctx0_o, lse0_o, ctx1_o, lse1_o, bias_s):
+    core, length = info[0], info[2]
+    rows, width = q.shape
+    pairs = width // LANES // 2
+    bias_s[...] = key_bias(core, length, rows)
+
+    def pair_step(shard, ctx_o, lse_o, local, carry):
+        pair = local + shard * pairs
+        cols = pl.ds(pl.multiple_of(pair * LANES, LANES), LANES)
+        vcols = pl.ds(pl.multiple_of(pair * LANES + width, LANES), LANES)
+        here = pl.ds(pl.multiple_of(local * LANES, LANES), LANES)
+        keys = jnp.concatenate([kvo[:, cols], kvf[:, cols]], axis=0).astype(jnp.float32)
+        vals = jnp.concatenate([kvo[:, vcols], kvf[:, vcols]], axis=0)
+        vals_t = turned(vals)
+        query = q[:, cols].astype(jnp.float32)
+        outs = []
+        for head in range(2):
+            in_k, extra_k = head_masks(2 * rows, head)
+            in_q, extra_q = head_masks(rows, head)
+            km = jnp.where(in_k, keys, jnp.where(extra_k, bias_s[...], 0.0)).astype(jnp.bfloat16)
+            qm = jnp.where(in_q, query, jnp.where(extra_q, 1.0, 0.0)).astype(jnp.bfloat16)
+            pieces = []
+            for start in range(0, rows, HALF):
+                scores = dot_nt(km, qm[start : start + HALF])
+                top = jnp.max(scores, axis=0, keepdims=True)
+                weights = jnp.exp(scores - top)
+                total = jnp.sum(weights, axis=0, keepdims=True)
+                out = dot_nn(
+                    vals_t[head * HEAD_DIM : (head + 1) * HEAD_DIM], weights.astype(jnp.bfloat16)
+                )
+                pieces.append(out / total)
+                lse_o[pl.ds(local * 2 + head, 1), start : start + HALF] = top + jnp.log(total)
+            outs.append(jnp.concatenate(pieces, axis=1))
+        ctx_o[:, here] = jnp.transpose(jnp.concatenate(outs, axis=0)).astype(jnp.bfloat16)
+        return carry
+
+    lax.fori_loop(0, pairs, functools.partial(pair_step, 0, ctx0_o, lse0_o), 0)
+    lax.fori_loop(0, pairs, functools.partial(pair_step, 1, ctx1_o, lse1_o), 0)
+
+
+def ffn_kernel(
+    info, resid_two, ctx0, ctx1, cot_own, cot_moved, gain, w_out, w_in, w_back, got2, part2,
+    got3, part3,
+    out_o, grad_three_o, gctx_o, ggain_o, send_o, keep_o,
+    wo_s, wi_s, wb_s, fin_s, fint_s, cot_s, acc_s, gacc_s, ctxt_s, n_s, sems,
+):
+    core, member = info[0], info[1]
+    loader = Loader(sems)
+    load_out(loader, w_out, got2, part2, core, wo_s)
+    load_in(loader, w_in, got2, part2, got3, part3, core, wi_s)
+    load_back(loader, w_back, got3, part3, core, wb_s)
+
+    @pl.when(core == member)
+    def _():
+        load_tiles(cot_own, n_s)
+
+    @pl.when(core != member)
+    def _():
+        load_tiles(cot_moved, n_s)
+
+    gather_rows(n_s, acc_s)
+    cot_s[...] = acc_s[...].astype(jnp.bfloat16)
+    loader.wait()
+    part = ctx0.shape[1]
+    chunks = wi_s.shape[0]
+    per_shard = chunks // 2
+    resid = resid_two[...] + dot_nn(ctx0[...], wo_s[0]) + dot_nn(ctx1[...], wo_s[1])
+    acc_s[...] = resid
+    gacc_s[...] = jnp.zeros_like(gacc_s)
+    unit, inv = row_stats(resid)
+    ffn_in = unit * gain[...]
+    fin_s[...] = ffn_in.astype(jnp.bfloat16)
+    fint_s[...] = jnp.transpose(fin_s[...].astype(jnp.float32)).astype(jnp.bfloat16)
+    keep_rows = pl.ds(pl.multiple_of(core * HALF, HALF), HALF)
+    send_rows = pl.ds(pl.multiple_of((1 - core) * HALF, HALF), HALF)
+
+    def chunk_step(index, carry):
+        shard, chunk = index // per_shard, index % per_shard
+        rows = pl.ds(pl.multiple_of(chunk * HALF, HALF), HALF)
+        into, back = wi_s[index], wb_s[shard, rows]
+        pre = dot_nn(fin_s[...], into)
+        sig = sigmoid(pre)
+        hidden = (pre * sig).astype(jnp.bfloat16)
+        acc_s[...] += dot_nn(hidden, back)
+        grad_hidden = dot_nt(cot_s[...], back)
+        grad_pre = (grad_hidden * (sig * (1.0 + pre * (1.0 - sig)))).astype(jnp.bfloat16)
+        send_o[shard, rows] = dot_nn(fint_s[send_rows], grad_pre).astype(jnp.bfloat16)
+        keep_o[shard, rows] = dot_nn(fint_s[keep_rows], grad_pre).astype(jnp.bfloat16)
+        hidden_t = turned(hidden)
+        base = per_shard * HALF
+        rows = pl.ds(pl.multiple_of(base + chunk * HALF, HALF), HALF)
+        send_o[shard, rows] = dot_nn(hidden_t, cot_s[:, send_rows]).astype(jnp.bfloat16)
+        keep_o[shard, rows] = dot_nn(hidden_t, cot_s[:, keep_rows]).astype(jnp.bfloat16)
+        gacc_s[...] += dot_nt(grad_pre, into)
+        return carry
+
+    lax.fori_loop(0, chunks, chunk_step, 0)
+    scatter_rows(acc_s, n_s, out_o)
+    unit, inv = row_stats(
+        resid_two[...] + dot_nn(ctx0[...], wo_s[0]) + dot_nn(ctx1[...], wo_s[1])
+    )
+    grad_norm = gacc_s[...]
+    ggain_o[...] = jnp.sum(grad_norm * unit, axis=0, keepdims=True)
+    grad_three = cot_s[...].astype(jnp.float32) + norm_grad(grad_norm, unit, inv, gain[...])
+    grad_three_o[...] = grad_three
+    fin_s[...] = grad_three.astype(jnp.bfloat16)
+    ctxt_s[:part] = turned(ctx0[...])
+    ctxt_s[part:] = turned(ctx1[...])
+    base = 2 * per_shard * HALF
+    for shard in range(2):
+        side = slice(shard * part, (shard + 1) * part)
+        gctx_o[:, side] = dot_nt(fin_s[...], wo_s[shard]).astype(jnp.bfloat16)
+        send_o[shard, base : base + part] = dot_nn(ctxt_s[side], fin_s[:, send_rows]).astype(
+            jnp.bfloat16
+        )
+        keep_o[shard, base : base + part] = dot_nn(ctxt_s[side], fin_s[:, keep_rows]).astype(
+            jnp.bfloat16
+        )
+
+
+def attend_back_kernel(
+    shard, info, q, kvo, kvf, ctx, gctx, lse, gq_o, gown_o, gfar_o, bias_s, gk_s, gv_s
+):
+    core, length = info[0], info[2]
+    rows, width = q.shape
+    pairs = width // LANES // 2
+    part = width // 2
+    scale = 1.0 / math.sqrt(HEAD_DIM)
+    bias_s[...] = key_bias(core, length, rows)
+
+    def pair_step(local, carry):
+        pair = local + shard * pairs
+        cols = pl.ds(pl.multiple_of(pair * LANES, LANES), LANES)
+        vcols = pl.ds(pl.multiple_of(pair * LANES + width, LANES), LANES)
+        here = pl.ds(pl.multiple_of(local * LANES, LANES), LANES)
+        vhere = pl.ds(pl.multiple_of(local * LANES + part, LANES), LANES)
+        keys = jnp.concatenate([kvo[:, cols], kvf[:, cols]], axis=0).astype(jnp.float32)
+        vals = jnp.concatenate([kvo[:, vcols], kvf[:, vcols]], axis=0)
+        keys_t = jnp.transpose(keys).astype(jnp.bfloat16)
+        query = q[:, cols].astype(jnp.float32)
+        grad_out = gctx[:, cols].astype(jnp.float32)
+        product_t = jnp.transpose(grad_out * ctx[:, here].astype(jnp.float32))
+        gk_s[...] = jnp.zeros_like(gk_s)
+        gv_s[...] = jnp.zeros_like(gv_s)
+        outs = []
+        for head in range(2):
+            in_k, extra_k = head_masks(2 * rows, head)
+            in_q, extra_q = head_masks(rows, head)
+            km = jnp.where(in_k, keys, jnp.where(extra_k, bias_s[...], 0.0)).astype(jnp.bfloat16)
+            qm = jnp.where(in_q, query, jnp.where(extra_q, 1.0, 0.0)).astype(jnp.bfloat16)
+            qz = jnp.where(in_q, query, 0.0).astype(jnp.bfloat16)
+            gz = jnp.where(in_q, grad_out, 0.0).astype(jnp.bfloat16)
+            span = slice(head * HEAD_DIM, (head + 1) * HEAD_DIM)
+            pieces = []
+            for start in range(0, rows, HALF):
+                at = slice(start, start + HALF)
+                level = lse[pl.ds(local * 2 + head, 1), at]
+                delta = jnp.sum(product_t[span, at], axis=0, keepdims=True)
+                soft = jnp.exp(dot_nt(km, qm[at]) - level)
+                gv_s[...] += dot_nn(soft.astype(jnp.bfloat16), gz[at])
+                grad_scores = (soft * (dot_nt(vals, gz[at]) - delta)).astype(jnp.bfloat16)
+                gk_s[...] += dot_nn(grad_scores, qz[at])
+                pieces.append(dot_nn(keys_t[span], grad_scores))
+            outs.append(jnp.concatenate(pieces, axis=1))
+        gq_o[:, here] = (jnp.transpose(jnp.concatenate(outs, axis=0)) * scale).astype(jnp.bfloat16)
+        gown_o[:, here] = gk_s[:rows]
+        gown_o[:, vhere] = gv_s[:rows]
+        gfar_o[:, here] = gk_s[rows:].astype(jnp.bfloat16)
+        gfar_o[:, vhere] = gv_s[rows:].astype(jnp.bfloat16)
+        return carry
+
+    lax.fori_loop(0, pairs, pair_step, 0)
+
+
+def qkv_part(shard, core, gq, gown, gfar, attn_in, w_s, attnt_s, send_o, keep_o):
+    attnt_s[...] = turned(attn_in[...])
+    width = w_s.shape[3]
+    keep_rows = pl.ds(pl.multiple_of(core * HALF, HALF), HALF)
+    send_rows = pl.ds(pl.multiple_of((1 - core) * HALF, HALF), HALF)
+    both = (gown[...] + gfar[...].astype(jnp.float32)).astype(jnp.bfloat16)
+    grad_in = None
+    for index, grad in enumerate((gq[...], both[:, :width], both[:, width:])):
+        at = slice(index * HALF, (index + 1) * HALF)
+        send_o[at] = dot_nn(attnt_s[send_rows], grad).astype(jnp.bfloat16)
+        keep_o[at] = dot_nn(attnt_s[keep_rows], grad).astype(jnp.bfloat16)
+        term = dot_nt(grad, w_s[shard, index])
+        grad_in = term if grad_in is None else grad_in + term
+    return grad_in
+
+
+def qkv_back_first(
+    info, gq, gown, gfar, attn_in, w_qkv, got, part, grad_o, send_o, keep_o, w_s, attnt_s, sems
+):
+    loader = Loader(sems)
+    load_qkv(loader, w_qkv, got, part, info[0], w_s, (0, 1, 2))
+    loader.wait()
+    grad_o[...] = qkv_part(1, info[0], gq, gown, gfar, attn_in, w_s, attnt_s, send_o, keep_o)
+
+
+def qkv_back_second(
+    info, gq, gown, gfar, attn_in, grad_part, resid_two, grad_three, gain, w_qkv, got, part,
+    grad_two_o, gsep_o, gedge_o, ggain_o, send_o, keep_o, w_s, attnt_s, n_s, sems,
+):
+    loader = Loader(sems)
+    load_qkv(loader, w_qkv, got, part, info[0], w_s, (0, 1, 2))
+    loader.wait()
+    grad_in = grad_part[...] + qkv_part(
+        0, info[0], gq, gown, gfar, attn_in, w_s, attnt_s, send_o, keep_o
+    )
+    unit, inv = row_stats(resid_two[...])
+    ggain_o[...] = jnp.sum(grad_in * unit, axis=0, keepdims=True)
+    grad_two = grad_three[...] + norm_grad(grad_in, unit, inv, gain[...])
+    grad_two_o[...] = grad_two
+    gsep_o[...] = grad_two[:, : gsep_o.shape[1]].astype(jnp.bfloat16)
+    rows = n_s.shape[1]
+    for tile, lanes in enumerate(lane_tiles(gsep_o.shape[1])):
+        n_s[tile] = grad_two[:, lanes]
+        first = n_s[tile, pl.ds(0, EDGE, stride=GROUP)]
+        last = n_s[tile, pl.ds(rows - EDGE * GROUP + GROUP - 1, EDGE, stride=GROUP)]
+        gedge_o[:, lanes] = jnp.where(info[0] == 0, last, first).astype(jnp.bfloat16)
+
+
+def point_kernel(info, gsep, depth, send0, keep0, send1, keep1, send_o, keep_o):
+    core = info[0]
+    grad_sep = gsep[...]
+    per_shard = depth.shape[0] // 2
+    per_core = per_shard // 2
+    base = send0.shape[0]
+    for shard, (send, keep) in enumerate(((send0, keep0), (send1, keep1))):
+        send_o[shard, :base] = send[...]
+        keep_o[shard, :base] = keep[...]
+        for chunk in range(per_core):
+            at = slice(base + chunk * HALF, base + (chunk + 1) * HALF)
+            first = shard * per_shard
+            send_o[shard, at] = dot_tn(
+                depth[first + (1 - core) * per_core + chunk], grad_sep
+            ).astype(jnp.bfloat16)
+            keep_o[shard, at] = dot_tn(
+                depth[first + core * per_core + chunk], grad_sep
+            ).astype(jnp.bfloat16)
+
+
+def as_f32(values):
+    return values.astype(jnp.float32)
+
+
+def slope_of(values):
+    sig = sigmoid(values)
+    return sig * (1.0 + values * (1.0 - sig))
+
+
+def depth_back_kernel(
+    info, gsep, gedge, left_pre, right_pre, stats, pack_own, w_point, got, part,
+    unit_o, scaled_o, sums_s, small_s,
+    wp_s, po_s, taps_s, gse_s, gd_s, din_s, near_s, unit_s, scaled_s, wide_s, sems,
+):
+    core, length = info[0], info[2]
+    loader = Loader(sems)
+    load_point(loader, w_point, got, part, core, wp_s)
+    load_pack(loader, got, part, core, po_s)
+    ext = left_pre.shape[1]
+    rows = ext - 2 * EDGE
+    chunks = left_pre.shape[0]
+    per_shard = chunks // 2
+    inner = chunks * HALF
+    sep_taps = pack_own.shape[0] - 1
+    right_cols = right_pre.shape[1]
+    stride = inner // right_cols
+    reach = sep_taps // 2
+    edge = gedge[...].astype(jnp.float32)
+    gse_s[:rows] = gsep[...]
+    gse_s[rows : rows + EDGE] = jnp.where(core == 1, edge, 0.0).astype(jnp.bfloat16)
+    gse_s[rows + EDGE :] = jnp.where(core == 1, 0.0, edge).astype(jnp.bfloat16)
+    wide_s[0] = row_mask(core, length, ext, LANES)
+    wide_s[1] = jnp.broadcast_to(stats[:, 0:1], (ext, LANES))
+    wide_s[2] = jnp.broadcast_to(stats[:, 1:2], (ext, LANES))
+    scaled_s[...] = jnp.zeros_like(scaled_s)
+    sums_s[...] = jnp.zeros_like(sums_s)
+    small_s[...] = jnp.zeros_like(small_s)
+    right_act = silu(right_pre[...]).astype(jnp.bfloat16)
+    loader.wait()
+    fill_taps(pack_own, po_s, taps_s)
+
+    def first(index, carry):
+        cols = pl.ds(pl.multiple_of(index * HALF, HALF), HALF)
+        taps = taps_s[:, cols]
+        shard, chunk = index // per_shard, index % per_shard
+        point = wp_s[shard, pl.ds(pl.multiple_of(chunk * HALF, HALF), HALF)]
+        grad_depth = dot_nt(gse_s[...], point)
+        for side, lanes in enumerate(lane_tiles(HALF)):
+            fill_window(gd_s.at[side], grad_depth[:, lanes], rows, reach)
+            near_s[side, :EDGE] = grad_depth[rows : rows + EDGE, lanes]
+            near_s[side, 3 * EDGE :] = grad_depth[rows + EDGE :, lanes]
+            base = reach * GROUP
+            near_s[side, EDGE : 2 * EDGE] = gd_s[side, pl.ds(base, EDGE, stride=GROUP)]
+            base = reach * GROUP + rows - EDGE * GROUP + GROUP - 1
+            near_s[side, 2 * EDGE : 3 * EDGE] = gd_s[side, pl.ds(base, EDGE, stride=GROUP)]
+        mid = silu(left_pre[index].astype(jnp.float32)) + dot_nn(
+            right_act, spread_block(index, HALF, stride)
+        )
+        for side in range(2):
+            lanes = slice(side * LANES, (side + 1) * LANES)
+            unit = (mid[:, lanes] - wide_s[1]) * wide_s[2]
+            unit_s[:, lanes] = unit
+            fill_window(
+                din_s.at[side],
+                unit * wide_s[0] * taps[sep_taps : sep_taps + 1, lanes],
+                rows,
+                reach,
+            )
+            for base, target in ((EDGE - GROUP, rows + EDGE - GROUP), (3 * EDGE, rows + EDGE)):
+                acc = near_s[side, base + reach : base + reach + GROUP] * taps[:1, lanes]
+                for tap in range(1, sep_taps):
+                    at = base + reach - tap
+                    acc = acc + near_s[side, at : at + GROUP] * taps[tap : tap + 1, lanes]
+                at = slice(target, target + GROUP)
+                scaled_s[at, lanes] = acc * wide_s[0, at]
+        step = 64
+        tap_sums = []
+        for side in range(2):
+            lanes = slice(side * LANES, (side + 1) * LANES)
+            sums = [jnp.zeros((GROUP, LANES), jnp.float32) for _ in range(sep_taps)]
+            for start in range(0, rows, step):
+                at = start + 2 * reach * GROUP
+                acc = gd_s[side, at : at + step] * taps[:1, lanes]
+                for tap in range(1, sep_taps):
+                    at = start + (2 * reach - tap) * GROUP
+                    acc = acc + gd_s[side, at : at + step] * taps[tap : tap + 1, lanes]
+                scaled_s[start : start + step, lanes] = acc * wide_s[0, start : start + step]
+                at = start + reach * GROUP
+                grad = gd_s[side, at : at + step]
+                for tap in range(sep_taps):
+                    at = start + tap * GROUP
+                    term = din_s[side, at : at + step] * grad
+                    sums[tap] = sums[tap] + jnp.sum(
+                        term.reshape(step // GROUP, GROUP, LANES), axis=0
+                    )
+            tap_sums.append(sums)
+        tap_sums = [jnp.concatenate(pair, axis=1) for pair in zip(*tap_sums)]
+        tap_rows = [jnp.sum(value, axis=0, keepdims=True) for value in tap_sums]
+        gain = taps[sep_taps : sep_taps + 1]
+        gain_row = jnp.sum(
+            scaled_s[:rows] * unit_s[:rows],
+            axis=0,
+            keepdims=True,
+        )
+        filler = jnp.zeros((small_s.shape[0] - sep_taps - 1, HALF), jnp.float32)
+        small_s[:, cols] = jnp.concatenate(tap_rows + [gain_row, filler], axis=0)
+        scaled = scaled_s[...] * gain
+        scaled_o[index] = scaled.astype(jnp.bfloat16)
+        unit_o[index] = unit_s[...].astype(jnp.bfloat16)
+        near, far = scaled[:, :LANES], scaled[:, LANES:]
+        sums_s[0] += near + far
+        sums_s[1] += near * unit_s[:, :LANES] + far * unit_s[:, LANES:]
+        return carry
+
+    lax.fori_loop(0, chunks, first, 0)
+
+
+def branch_back_kernel(
+    info, unit, scaled, sums, small, left_pre, right_pre, stats, branch, gain_ffn_g, gain_attn_g,
+    gleft_o, gright_o, send_o, keep_o,
+    wide_s, gra_s, bt_s,
+):
+    core = info[0]
+    ext = left_pre.shape[1]
+    rows = ext - 2 * EDGE
+    chunks = left_pre.shape[0]
+    per_shard = chunks // 2
+    inner = chunks * HALF
+    right_cols = right_pre.shape[1]
+    stride = inner // right_cols
+    for index in range(2):
+        mean = jnp.sum(sums[index], axis=-1, keepdims=True) / inner
+        wide_s[index] = jnp.broadcast_to(mean, (ext, LANES))
+    wide_s[2] = jnp.broadcast_to(stats[:, 1:2], (ext, LANES))
+    gra_s[...] = jnp.zeros_like(gra_s)
+    bt_s[...] = turned(branch[...])
+    keep_rows = pl.ds(pl.multiple_of(core * HALF, HALF), HALF)
+    send_rows = pl.ds(pl.multiple_of((1 - core) * HALF, HALF), HALF)
+
+    def second(index, carry):
+        shard, chunk = index // per_shard, index % per_shard
+        sides = []
+        for side in range(2):
+            lanes = slice(side * LANES, (side + 1) * LANES)
+            sides.append(
+                wide_s[2]
+                * (as_f32(scaled[index, :, lanes]) - wide_s[0] - as_f32(unit[index, :, lanes]) * wide_s[1])
+            )
+        grad_mid = jnp.concatenate(sides, axis=1)
+        grad_left = (
+            grad_mid[:rows] * slope_of(left_pre[index, :rows].astype(jnp.float32))
+        ).astype(jnp.bfloat16)
+        gleft_o[index] = grad_left
+        gra_s[...] += dot_nt(grad_mid.astype(jnp.bfloat16), spread_block(index, HALF, stride))
+        at = pl.ds(pl.multiple_of(chunk * HALF, HALF), HALF)
+        send_o[shard, at] = dot_nn(bt_s[send_rows, :rows], grad_left).astype(
+            jnp.bfloat16
+        )
+        keep_o[shard, at] = dot_nn(bt_s[keep_rows, :rows], grad_left).astype(
+            jnp.bfloat16
+        )
+        return carry
+
+    lax.fori_loop(0, chunks, second, 0)
+    grad_right = gra_s[...] * slope_of(right_pre[...])
+    gright_o[...] = grad_right.astype(jnp.bfloat16)
+    spot = lax.broadcasted_iota(jnp.int32, grad_right.shape, 0)
+    own_right = jnp.where(spot < rows, grad_right, 0.0)
+    part = right_cols // 2
+    base = per_shard * HALF
+    for target, picked, side in ((send_o, send_rows, 1 - core), (keep_o, keep_rows, core)):
+        taps3 = []
+        for tap in range(3):
+            moved = shift_rows(own_right, 1 - tap).astype(jnp.bfloat16)
+            taps3.append(dot_nn(bt_s[picked, :], moved).astype(jnp.bfloat16))
+        for shard in range(2):
+            cols = slice(shard * part, (shard + 1) * part)
+            target[shard, base : base + HALF, :part] = taps3[0][:, cols]
+            target[shard, base : base + HALF, part:] = taps3[1][:, cols]
+            target[shard, base + HALF : base + 2 * HALF, :part] = taps3[2][:, cols]
+            target[shard, base + HALF : base + 2 * HALF, part:] = jnp.zeros(
+                (HALF, part), jnp.bfloat16
+            )
+            cols_here = inner // 4
+            for piece in range(cols_here // LANES):
+                lanes = pl.ds(
+                    pl.multiple_of(
+                        shard * (inner // 2) + side * cols_here + piece * LANES, LANES
+                    ),
+                    LANES,
+                )
+                row = base + HALF + piece * 16
+                target[shard, row : row + 16, part:] = small[:, lanes].astype(jnp.bfloat16)
+            row = base + HALF + 4 * 16
+            for piece in range(4):
+                lanes = slice(piece * LANES, (piece + 1) * LANES)
+                both = jnp.concatenate(
+                    [gain_ffn_g[:, lanes], gain_attn_g[:, lanes], jnp.zeros((14, LANES), jnp.float32)],
+                    axis=0,
+                )
+                target[shard, row : row + 16, part:] = both.astype(jnp.bfloat16)
+                row += 16
+
+
+def join_back_kernel(
+    info, gleft, gright, resid_one, grad_two, gain_branch, w_left, w_right, got, part_w,
+    grad_one_o, ggain_o, wl_s, wr_s, sems,
+):
+    core, length = info[0], info[2]
+    loader = Loader(sems)
+    load_left(loader, w_left, got, part_w, core, wl_s)
+    load_right(loader, w_right, got, part_w, core, wr_s)
+    ext = gright.shape[0]
+    rows = ext - 2 * EDGE
+    own = slice(0, rows)
+    loader.wait()
+    grad_in = jnp.zeros((rows, resid_one.shape[1]), jnp.float32)
+    for index in range(wl_s.shape[0]):
+        grad_in = grad_in + dot_nt(gleft[index], wl_s[index])
+    part = wr_s.shape[3]
+    for tap in range(wr_s.shape[1]):
+        product = dot_nt(gright[:, :part], wr_s[0, tap]) + dot_nt(gright[:, part:], wr_s[1, tap])
+        grad_in = grad_in + shift_rows(product, 1 - tap)[own]
+    grad_in = grad_in * row_mask(core, length, ext, LANES)[own, :1]
+    unit, inv = row_stats(resid_one[own])
+    ggain_o[...] = jnp.sum(grad_in * unit, axis=0, keepdims=True)
+    grad_one_o[...] = grad_two[...] + norm_grad(grad_in, unit, inv, gain_branch[...])
+
+
+def glu_back_kernel(
+    info, grad_one, gain_branch_row, gain_glu, block, moved, glu_in, value, sig, w_value, w_gate,
+    got, part_w,
+    gin_o, send_o, keep_o,
+    wv_s, wg_s, x_s, n_s, git_s, sems,
+):
+    core, member = info[0], info[1]
+    loader = Loader(sems)
+    load_pair(loader, w_value, got, part_w, 0, core, wv_s, (member, 1 - member))
+    load_pair(loader, w_gate, got, part_w, 1, core, wg_s, (member, 1 - member))
+    rows = grad_one.shape[0]
+    own = slice(0, rows)
+
+    @pl.when(core == member)
+    def _():
+        load_tiles(block, n_s)
+
+    @pl.when(core != member)
+    def _():
+        load_tiles(moved, n_s)
+
+    gather_rows(n_s, x_s)
+    git_s[...] = turned(glu_in[own])
+    loader.wait()
+    grad_glu = grad_one[...].astype(jnp.bfloat16).astype(jnp.float32)
+    keep_rows = pl.ds(pl.multiple_of(core * HALF, HALF), HALF)
+    send_rows = pl.ds(pl.multiple_of((1 - core) * HALF, HALF), HALF)
+    grad_norm = jnp.zeros(grad_one.shape, jnp.float32)
+    for half in range(2):
+        cols = slice(half * HALF, (half + 1) * HALF)
+        sig_f = sig[own, cols].astype(jnp.float32)
+        grad_here = grad_glu[:, cols] * sig_f
+        grad_value = grad_here.astype(jnp.bfloat16)
+        grad_gate = (grad_here * value[own, cols].astype(jnp.float32) * (1.0 - sig_f)).astype(
+            jnp.bfloat16
+        )
+        slot = jnp.where(member == half, 0, 1)
+        send_o[slot, :HALF] = dot_nn(git_s[send_rows], grad_value).astype(jnp.bfloat16)
+        keep_o[slot, :HALF] = dot_nn(git_s[keep_rows], grad_value).astype(jnp.bfloat16)
+        send_o[slot, HALF : 2 * HALF] = dot_nn(git_s[send_rows], grad_gate).astype(jnp.bfloat16)
+        keep_o[slot, HALF : 2 * HALF] = dot_nn(git_s[keep_rows], grad_gate).astype(jnp.bfloat16)
+        grad_norm = grad_norm + dot_nt(grad_value, wv_s[half]) + dot_nt(grad_gate, wg_s[half])
+    unit, inv = row_stats(x_s[...])
+    gain_glu_row = jnp.sum(grad_norm * unit, axis=0, keepdims=True)
+    x_s[...] = grad_one[...] + norm_grad(grad_norm, unit, inv, gain_glu[...])
+    scatter_rows(x_s, n_s, gin_o)
+    tail = send_o.shape[1] - 2 * HALF
+    both = jnp.concatenate(
+        [gain_glu_row, gain_branch_row[...], jnp.zeros((14, 2 * HALF), jnp.float32)], axis=0
+    )
+    both = both.astype(jnp.bfloat16)
+    for target in (send_o, keep_o):
+        for shard in range(2):
+            target[shard, 2 * HALF :] = jnp.zeros((tail, HALF), jnp.bfloat16)
+            target[shard, 2 * HALF : 2 * HALF + 16] = both[:, :HALF]
+            target[shard, 2 * HALF + 16 : 2 * HALF + 32] = both[:, HALF:]
+
+
+def over_mp(values):
+    return lax.ppermute(values, "mp", [(0, 1), (1, 0)])
+
+
+def flat_pairs(dp_size, rule):
+    pairs = []
+    for dp_index in range(dp_size):
+        for member in range(2):
+            pair, core = dp_index // 2, dp_index % 2
+            new_core, new_member = rule(core, member)
+            pairs.append((dp_index * 2 + member, (pair * 2 + new_core) * 2 + new_member))
+    return pairs
+
+
+def unpack_kernel(layout, halves, info, both, far, *rest):
+    outs, packed, sems = rest[:-2], rest[-2], rest[-1]
+    core, ybit, zpos = info[0], info[3], info[4]
+    ys, zs, step = both.shape[0], 4, both.shape[3]
+    loader = Loader(sems)
+    for half in range(2):
+        for yside in range(ys):
+            for zside in range(zs):
+                at = (yside ^ ybit, zside // 2 ^ zpos % 2, zside % 2 ^ zpos // 2)
+                first, base = 0, 0
+                for size in halves:
+                    low = max(first, zside * step)
+                    top = min(first + size, (zside + 1) * step)
+                    if low < top:
+                        source = pl.ds(low - zside * step, top - low)
+                        target = packed.at[
+                            half, pl.ds(base + yside * size + low - first, top - low)
+                        ]
+                        loader.either(
+                            both.at[at].at[source], far.at[at].at[source], core == half, target
+                        )
+                    first += size
+                    base += 2 * size
+    loader.wait()
+    layout(packed, outs)
+
+
+def layout_early(packed, outs):
+    layout_attn(packed, outs[:2])
+    w_in, w_back, w_out = outs[2:]
+    blocks = w_in.shape[1] // HALF
+    first = 5 * HALF
+    base = first + blocks * HALF
+    for half in range(2):
+        side = slice(half * HALF, (half + 1) * HALF)
+        for block in range(blocks):
+            at = first + block * HALF
+            w_in[side, block * HALF : (block + 1) * HALF] = as_f32(packed[half, at : at + HALF])
+        w_back[:, side] = as_f32(packed[half, base : base + w_back.shape[0]])
+        last = base + w_back.shape[0]
+        w_out[:, side] = as_f32(packed[half, last : last + w_out.shape[0]])
+
+
+def layout_attn(packed, outs):
+    w_qkv, w_point = outs
+    for half in range(2):
+        for index in range(3):
+            w_qkv[index, half * HALF : (half + 1) * HALF] = as_f32(
+                packed[half, index * HALF : (index + 1) * HALF]
+            )
+        w_point[half * 2 * HALF : (half + 1) * 2 * HALF] = as_f32(
+            packed[half, 3 * HALF : 5 * HALF]
+        )
+
+
+def layout_branch(packed, outs):
+    w_left, w_right, pack, gains = outs
+    blocks = w_left.shape[1] // HALF
+    base = blocks * HALF
+    for half in range(2):
+        side = slice(half * HALF, (half + 1) * HALF)
+        for block in range(blocks):
+            w_left[side, block * HALF : (block + 1) * HALF] = as_f32(
+                packed[half, block * HALF : (block + 1) * HALF]
+            )
+        w_right[0, side] = as_f32(packed[half, base : base + HALF, :LANES])
+        w_right[1, side] = as_f32(packed[half, base : base + HALF, LANES:])
+        w_right[2, side] = as_f32(packed[half, base + HALF : base + 2 * HALF, :LANES])
+        for piece in range(4):
+            row = base + HALF + piece * 16
+            at = half * 4 * LANES + piece * LANES
+            pack[:, at : at + LANES] = as_f32(packed[half, row : row + 16, LANES:])
+            row += 4 * 16
+            gains[:, piece * LANES : (piece + 1) * LANES] = as_f32(
+                packed[half, row : row + 16, LANES:]
+            )
+
+
+def layout_glu(packed, outs):
+    w_value, w_gate, gains = outs
+    for half in range(2):
+        side = slice(half * HALF, (half + 1) * HALF)
+        w_value[side] = as_f32(packed[half, :HALF])
+        w_gate[side] = as_f32(packed[half, HALF : 2 * HALF])
+        gains[:, side] = as_f32(packed[0, 2 * HALF + 16 * half : 2 * HALF + 16 * (half + 1)])
+
+
+VMEM_LIMIT = 56 * 1024 * 1024
+
+
+def call(body, name, ins, outs, scratch, flops, copies=0):
+    spaces = {"s": pltpu.SMEM, "v": pltpu.VMEM, "h": pl.ANY}
+    shapes = [jax.ShapeDtypeStruct(shape, dtype) for shape, dtype in outs]
+    scratch = [pltpu.VMEM(shape, dtype) for shape, dtype in scratch]
+    if copies:
+        scratch.append(pltpu.SemaphoreType.DMA((copies,)))
+    return pl.pallas_call(
+        body,
+        out_shape=shapes,
+        in_specs=[pl.BlockSpec(memory_space=spaces[place]) for _, place in ins],
+        out_specs=[pl.BlockSpec(memory_space=pltpu.VMEM) for _ in shapes],
+        scratch_shapes=scratch,
+        name=name,
+        compiler_params=pltpu.CompilerParams(vmem_limit_bytes=VMEM_LIMIT),
+        cost_estimate=pl.CostEstimate(flops=10**10, bytes_accessed=10**6, transcendentals=0),
+    )(*[array for array, _ in ins])
+
+
+def dp_xor(values, bits):
+    size = lax.axis_size("dp")
+    return lax.ppermute(values, "dp", [(index, index ^ bits) for index in range(size)])
+
+
+def over_x_and_y(values):
+    pairs = []
+    for dp_index in range(lax.axis_size("dp")):
+        for member in range(2):
+            pairs.append((dp_index * 2 + member, (dp_index ^ 2) * 2 + 1 - member))
+    return lax.ppermute(values, ("dp", "mp"), pairs)
+
+
+def in_blocks(values):
+    return [values[:, at : at + HALF] for at in range(0, values.shape[1], HALF)]
+
+
+def bundle_branch(core, w_left, w_right, w_point, pack):
+    depth = 16
+    pack = jnp.pad(pack, ((0, depth - pack.shape[0]), (0, 0)))
+    first = jnp.concatenate(in_blocks(w_left) + in_blocks(pack), axis=0)
+    blank = jnp.zeros_like(w_right[0])
+    second = [
+        w_point,
+        jnp.concatenate([w_right[0], w_right[1]], axis=1),
+        jnp.concatenate([w_right[2], blank], axis=1),
+        jnp.zeros((first.shape[0] - w_point.shape[0] - 2 * blank.shape[0], HALF), first.dtype),
+    ]
+    return jnp.where(core == 0, first, jnp.concatenate(second, axis=0))
+
+
+def bundle_attn(core, w_qkv, w_out, w_in):
+    first = w_qkv.reshape(-1, HALF)
+    return jnp.where(core == 0, first, jnp.concatenate(in_blocks(w_out) + in_blocks(w_in)[:2], axis=0))
+
+
+def bundle_ffn(core, w_in, w_back):
+    half = w_back.shape[0] // 2
+    near, far = in_blocks(w_back)
+    first = jnp.concatenate([near, far[:half]], axis=0)
+    return jnp.where(core == 0, first, jnp.concatenate([far[half:]] + in_blocks(w_in)[2:], axis=0))
+
+
+def later(values, *first):
+    return lax.optimization_barrier((values, first))[0]
+
+
+class Sums:
+    def __init__(self, send, keep, ybit):
+        self.keep, self.ybit = keep, ybit
+        self.recv = dp_xor(send, 1)
+
+    def over_xy(self, *first):
+        recv, keep = later((self.recv, self.keep), *first)
+        half = keep.shape[1] // 2
+
+        def piece(shard, bit):
+            at = bit * half
+            cut = lambda values: as_f32(lax.dynamic_slice_in_dim(values[shard], at, half, axis=0))
+            return (cut(keep) + cut(recv)).astype(jnp.bfloat16)
+
+        self.kept = piece(0, self.ybit)
+        gone = [piece(1, self.ybit), piece(0, 1 - self.ybit), piece(1, 1 - self.ybit)]
+        self.got = [over_mp(gone[0]), dp_xor(gone[1], 2), over_x_and_y(gone[2])]
+        return gone
+
+    def quarter(self, *first):
+        got, kept = later((self.got, self.kept), *first)
+        total = as_f32(kept) + as_f32(got[1]) + (as_f32(got[0]) + as_f32(got[2]))
+        return total.astype(jnp.bfloat16)
+
+
+class Rest:
+    def __init__(self, quarters, zpos):
+        self.quarters, self.zpos = quarters, zpos
+
+    def over_z1(self, *first):
+        mine = jnp.concatenate(later(self.quarters, *first), axis=0)
+        return self.halve(mine, self.zpos % 2, 4)
+
+    def over_z2(self, *first):
+        got, kept = later((self.got, self.kept), *first)
+        mine = (as_f32(kept) + as_f32(got)).astype(jnp.bfloat16)
+        return self.halve(mine, self.zpos // 2, 8)
+
+    def halve(self, mine, bit, across):
+        half = mine.shape[0] // 2
+        self.kept = lax.dynamic_slice_in_dim(mine, bit * half, half, axis=0)
+        gone = lax.dynamic_slice_in_dim(mine, (1 - bit) * half, half, axis=0)
+        self.got = dp_xor(gone, across)
+        return [gone]
+
+    def back_z2(self, *first):
+        got, kept = later((self.got, self.kept), *first)
+        self.mine = (as_f32(kept) + as_f32(got)).astype(jnp.bfloat16)
+        self.got = dp_xor(self.mine, 8)
+        return [self.mine]
+
+    def back_z1(self, *first):
+        return self.double(4, *first)
+
+    def double(self, across, *first):
+        got, mine = later((self.got, self.mine), *first)
+        self.mine = jnp.stack([mine, got])
+        self.got = dp_xor(self.mine, across)
+        return [self.mine]
+
+    def back_y(self, *first):
+        return self.double(2, *first)
+
+    def back_core(self, *first):
+        self.got, mine = later((self.got, self.mine), *first)
+        self.both = jnp.stack([mine, self.got])
+        self.far = dp_xor(self.both, 1)
+        return [self.both]
+
+
+def unpack(layout, info, sums, outs):
+    ys, zs, part, cols = 2, 4, *sums.both.shape[3:]
+    halves = [quarter.shape[0] for quarter in sums.quarters]
+    return call(
+        functools.partial(unpack_kernel, layout, halves),
+        "unpack_" + layout.__name__,
+        [(info, "s"), (sums.both, "h"), (sums.far, "h")],
+        [(shape, jnp.float32) for shape in outs],
+        [((2, ys * zs * part, cols), jnp.bfloat16)],
+        1e6,
+        2 * ys * (zs + len(halves)),
+    )
+
+
+def paired(
+    inputs, lengths, gain_glu, w_value, w_gate, gain_branch, w_left, w_right, gain_mid, w_depth,
+    w_point, gain_attn, w_qkv, w_out, gain_ffn, w_in, w_back, cotangent,
+):
+    low, full = jnp.bfloat16, jnp.float32
+    member = lax.axis_index("mp")
+    place = lax.axis_index("dp")
+    core, ybit, zpos = place % 2, (place // 2) % 2, place // 4
+    rows, width = inputs.shape[1:]
+    ext = rows + 2 * EDGE
+    inner = 2 * w_left.shape[1]
+    chunks = inner // HALF
+    right_cols = 2 * w_right.shape[2]
+    sep_width = w_point.shape[1]
+    heads = 2 * w_qkv.shape[2] // HEAD_DIM
+    row = lambda gain: gain.reshape(1, -1)
+
+    block = inputs[0]
+    edge = jnp.where(member == 0, block[rows - EDGE :], block[:EDGE])
+    size_code = jnp.stack([lengths[0] // 32, lengths[0] % 32]).astype(low)
+    code_rows = jnp.broadcast_to(jnp.repeat(size_code, EDGE // 2)[:, None], (EDGE, width))
+    edge = jnp.concatenate([edge, code_rows], axis=0)
+    edge = lax.ppermute(
+        edge, ("dp", "mp"), flat_pairs(lax.axis_size("dp"), lambda c, m: (1 - m, c))
+    )
+    code = as_f32(edge[EDGE:, 0])
+    length = (code[0] * 32 + code[EDGE // 2]).astype(jnp.int32)
+    edge = edge[:EDGE]
+    swap = [p for p in flat_pairs(lax.axis_size("dp"), lambda c, m: (m, c)) if p[0] != p[1]]
+    moved = lax.ppermute(block, ("dp", "mp"), swap)
+    info = jnp.stack([core, member, length, ybit, zpos]).astype(jnp.int32)
+
+    pack = jnp.concatenate([w_depth, gain_mid[None]], axis=0)
+    got0 = over_mp(jnp.where(core == 0, w_value, w_gate))
+    bundle = later(
+        bundle_branch(core, w_left, w_right, w_point, pack), edge
+    )
+    got1 = over_mp(bundle)
+    part0 = dp_xor(later(got0, bundle), 1)
+    got2 = over_mp(later(bundle_attn(core, w_qkv, w_out, w_in), got0, moved))
+    cot = cotangent[0]
+    cot_moved = lax.ppermute(later(cot, got0, moved), ("dp", "mp"), swap)
+
+    v = lambda *arrays: [(array, "v") for array in arrays]
+    h = lambda *arrays: [(array, "h") for array in arrays]
+    where = [(info, "s")]
+    macs = 2.0 * rows * width
+    resid_one, branch_in, glu_in, value, sig = call(
+        glu_kernel, "glu",
+        where + v(block, moved, edge, row(gain_glu), row(gain_branch))
+        + h(w_value, w_gate, got0, part0),
+        [((ext, width), full)] + [((ext, width), low)] * 4,
+        [((ext, width), full), ((width // LANES, rows, LANES), full)]
+        + [((2,) + w_value.shape, low)] * 2,
+        macs * width * 2, 8,
+    )
+    got1 = later(got1, glu_in)
+    part1 = dp_xor(got1, 1)
+    got2 = later(got2, got1)
+    part2 = dp_xor(got2, 1)
+    got3 = over_mp(later(bundle_ffn(core, w_in, w_back), got1))
+    resid_two, left_pre, right_pre, stats, depth = call(
+        branch_kernel, "branch",
+        where + v(branch_in, resid_one, pack) + h(w_left, w_right, w_point, got1, part1),
+        [
+            ((rows, width), full), ((chunks, ext, HALF), low), ((ext, right_cols), full),
+            ((ext, LANES), full), ((chunks, rows, HALF), low),
+        ],
+        [
+            ((chunks, width, HALF), low), ((2,) + w_right.shape, low), ((2,) + w_point.shape, low),
+            ((4, 16, HALF), low), ((16, inner), full), ((chunks, ext, HALF), full),
+            ((rows + 64, HALF), full),
+            ((2, ext, LANES), full), ((rows, sep_width), full),
+        ],
+        macs * 8000, 20,
+    )
+    attn_in, kv_own = call(
+        kv_kernel, "keys_values",
+        where + v(resid_two, row(gain_attn)) + h(w_qkv, got2, part2),
+        [((rows, width), low), ((rows, 2 * width), low)],
+        [((2, 2) + w_qkv.shape[1:], low)],
+        macs * width * 2, 8,
+    )
+    (queries,) = call(
+        query_kernel, "queries",
+        where + v(attn_in) + h(w_qkv, got2, part2),
+        [((rows, width), low)],
+        [((2, 1) + w_qkv.shape[1:], low)],
+        macs * width, 4,
+    )
+    kv_far = dp_xor(kv_own, 1)
+    context0, lse0, context1, lse1 = call(
+        attend_kernel, "attend",
+        [(later(info, cot_moved), "s")] + v(queries, kv_own, kv_far),
+        [((rows, width // 2), low), ((heads // 2, rows), full)] * 2,
+        [((2 * rows, LANES), full)],
+        macs * 8000,
+    )
+    part3 = dp_xor(later(got3, lse1), 1)
+    r_ffn = 2 * w_in.shape[1] + w_out.shape[0]
+    out_rows, grad_three, grad_ctx, ggain_ffn, send, keep = call(
+        ffn_kernel, "ffn",
+        where + v(resid_two, context0, context1, cot, cot_moved, row(gain_ffn))
+        + h(w_out, w_in, w_back, got2, part2, got3, part3),
+        [
+            ((rows, width), low), ((rows, width), full), ((rows, width), low), ((1, width), full),
+            ((2, r_ffn, HALF), low), ((2, r_ffn, HALF), low),
+        ],
+        [
+            ((2,) + w_out.shape, low), ((chunks, width, HALF), low), ((2,) + w_back.shape, low),
+            ((rows, width), low), ((width, rows), low), ((rows, width), low), ((rows, width), full),
+            ((rows, width), full), ((width, rows), low), ((width // LANES, rows, LANES), full),
+        ],
+        macs * 16000, 24,
+    )
+    ffn_sums = Sums(send, keep, ybit)
+    swapped_out = lax.ppermute(out_rows, ("dp", "mp"), swap)
+
+    def attend_back(shard, info, context, lse):
+        return call(
+            functools.partial(attend_back_kernel, shard), "attend_back",
+            [(info, "s")] + v(queries, kv_own, kv_far, context, grad_ctx, lse),
+            [((rows, width // 2), low), ((rows, width), full), ((rows, width), low)],
+            [((2 * rows, LANES), full)] * 3,
+            macs * 10000,
+        )
+
+    grad_q1, grad_own1, grad_far1 = attend_back(1, info, context1, lse1)
+    recv1 = dp_xor(grad_far1, 1)
+    sent = ffn_sums.over_xy(grad_q1)
+    grad_q0, grad_own0, grad_far0 = attend_back(0, later(info, *sent), context0, lse0)
+    recv0 = dp_xor(grad_far0, 1)
+    parts = [((3 * HALF, HALF), low)] * 2
+    scratch = [((2,) + w_qkv.shape, low), ((width, rows), low)]
+    grad_part, send1, keep1 = call(
+        qkv_back_first, "qkv_back_first",
+        where + v(grad_q1, grad_own1, recv1, attn_in) + h(w_qkv, got2, part2),
+        [((rows, width), full)] + parts, scratch, macs * 3000, 12,
+    )
+    grad_two, grad_sep, sep_edge, ggain_attn, send0, keep0 = call(
+        qkv_back_second, "qkv_back_second",
+        where
+        + v(
+            grad_q0, grad_own0, recv0, attn_in, grad_part, resid_two, grad_three, row(gain_attn)
+        )
+        + h(w_qkv, got2, part2),
+        [
+            ((rows, width), full), ((rows, sep_width), low), ((EDGE, sep_width), low),
+            ((1, width), full),
+        ]
+        + parts,
+        scratch + [((sep_width // LANES, rows, LANES), full)], macs * 3000, 12,
+    )
+    sep_edge = dp_xor(sep_edge, 1)
+    send, keep = call(
+        point_kernel, "point_back",
+        where + v(grad_sep, depth, send0, keep0, send1, keep1),
+        [((2, 5 * HALF, HALF), low)] * 2, [], macs * 1000,
+    )
+    attn_sums = Sums(send, keep, ybit)
+    ffn_quarter = ffn_sums.quarter(send)
+    sent = [ffn_quarter]
+    unit, scaled, mid_sums, small = call(
+        depth_back_kernel, "depth_back",
+        [(later(info, *sent), "s")]
+        + v(grad_sep, sep_edge, left_pre, right_pre, stats, pack)
+        + h(w_point, got1, part1),
+        [
+            ((chunks, ext, HALF), low), ((chunks, ext, HALF), low), ((2, ext, LANES), full),
+            ((16, inner), full),
+        ],
+        [
+            ((2,) + w_point.shape, low), ((4, 16, HALF), low), ((16, inner), full),
+            ((ext, sep_width), low),
+            ((2, rows + 64, LANES), full), ((2, rows + 64, LANES), full),
+            ((2, 4 * EDGE, LANES), full), ((ext, HALF), full), ((ext, HALF), full),
+            ((3, ext, LANES), full),
+        ],
+        macs * 8000, 8,
+    )
+    sent = attn_sums.over_xy(mid_sums)
+    r_branch = inner // 2 + 2 * HALF
+    grad_left, grad_right, send, keep = call(
+        branch_back_kernel, "branch_back",
+        [(later(info, *sent), "s")]
+        + v(
+            unit, scaled, mid_sums, small, left_pre, right_pre, stats, branch_in, ggain_ffn,
+            ggain_attn,
+        ),
+        [
+            ((chunks, rows, HALF), low), ((ext, right_cols), low),
+            ((2, r_branch, HALF), low), ((2, r_branch, HALF), low),
+        ],
+        [((3, ext, LANES), full), ((ext, right_cols), full), ((width, ext), low)],
+        macs * 4000,
+    )
+    branch_sums = Sums(send, keep, ybit)
+    early = Rest([attn_sums.quarter(grad_left), ffn_quarter], zpos)
+    sent = early.over_z1(grad_left)
+    grad_one, ggain_branch = call(
+        join_back_kernel, "join_back",
+        [(later(info, *sent), "s")]
+        + v(grad_left, grad_right, resid_one, grad_two, row(gain_branch))
+        + h(w_left, w_right, got1, part1),
+        [((rows, width), full), ((1, width), full)],
+        [((chunks, width, HALF), low), ((2,) + w_right.shape, low)],
+        macs * 4000, 12,
+    )
+    sent = branch_sums.over_xy(grad_one)
+    grad_in, send, keep = call(
+        glu_back_kernel, "glu_back",
+        [(later(info, *sent), "s")]
+        + v(grad_one, ggain_branch, row(gain_glu), block, moved, glu_in, value, sig)
+        + h(w_value, w_gate, got0, part0),
+        [((rows, width), low), ((2, 640, HALF), low), ((2, 640, HALF), low)],
+        [
+            ((2,) + w_value.shape, low), ((2,) + w_gate.shape, low), ((rows, width), full),
+            ((width // LANES, rows, LANES), full), ((width, rows), low),
+        ],
+        macs * 3000, 4,
+    )
+    glu_sums = Sums(send, keep, ybit)
+    swapped_in = lax.ppermute(grad_in, ("dp", "mp"), swap)
+    sent = early.over_z2(grad_in)
+    sent = glu_sums.over_xy(*sent)
+    branch_rest = Rest([branch_sums.quarter(*sent)], zpos)
+    sent = branch_rest.over_z1(*sent)
+    glu_rest = Rest([glu_sums.quarter(*sent)], zpos)
+    sent = glu_rest.over_z1(*sent)
+    sent = early.back_z2(*sent)
+    sent = branch_rest.over_z2(*sent)
+    sent = glu_rest.over_z2(*sent)
+    sent = early.back_z1(*sent)
+    sent = branch_rest.back_z2(*sent)
+    sent = glu_rest.back_z2(*sent)
+    sent = early.back_y(*sent)
+    sent = branch_rest.back_z1(*sent)
+    sent = glu_rest.back_z1(*sent)
+    sent = early.back_core(*sent)
+    sent = branch_rest.back_y(*sent)
+    sent = glu_rest.back_y(*sent)
+    outputs = jnp.where(member == core, out_rows, swapped_out)
+    grad_inputs = jnp.where(member == core, grad_in, swapped_in)
+    g_qkv, g_point, g_in, g_back, g_out = unpack(
+        layout_early, later(info, *sent), early,
+        [w_qkv.shape, w_point.shape, w_in.shape, w_back.shape, w_out.shape],
+    )
+    sent = branch_rest.back_core(g_qkv)
+    sent = glu_rest.back_core(*sent)
+    g_left, g_right, g_pack, g_late = unpack(
+        layout_branch, later(info, *sent), branch_rest,
+        [w_left.shape, w_right.shape, (16, inner // 2), (16, width)],
+    )
+    g_value, g_gate, g_last = unpack(
+        layout_glu, info, glu_rest, [w_value.shape, w_gate.shape, (16, width)]
+    )
+    taps = w_depth.shape[0]
+    return (
+        outputs[None],
+        grad_inputs[None],
+        g_last[0],
+        g_value,
+        g_gate,
+        g_last[1],
+        g_left,
+        g_right,
+        g_pack[taps],
+        g_pack[:taps],
+        g_point,
+        g_late[1],
+        g_qkv,
+        g_out,
+        g_late[0],
+        g_in,
+        g_back,
+    )
+
+
 def solution(mesh):
     placed = (
         P("dp", "mp", None),
@@ -466,8 +1943,9 @@
         P("mp", None),
         P("dp", "mp", None),
     )
+    fast = mesh.shape["mp"] == 2 and mesh.shape["dp"] == 16
     return jax.shard_map(
-        local,
+        paired if fast else local,
         mesh=mesh,
         in_specs=placed,
         out_specs=(

time: 703 us -> 363 us (0.52)
  waiting for transfers between devices: 286 us -> 118 us
  Pallas kernels: 0 us -> 151 us
  matrix products: 118 us -> 0 us
  blocking collectives: 118 us -> 0 us
  other arithmetic: 99.1 us -> 12.6 us
  starting transfers between devices: 9.96 us -> 46.9 us
  local copies, waits for them, and re-layouts: 47.4 us -> 22.9 us
  between operations: 16 us -> 3.98 us
    pallas_call x0 -> x18, Pallas kernels: none -> 151 us  [call(): pl.pallas_call(body, out_shape=shapes, in_specs=[pl.BlockSpec(memory_spac...]
    all_gather x6 -> x0, waiting for transfers between devices: 124 us -> none  [spread_rows(): return lax.all_gather(pieces, 'mp', axis=1, tiled=True)]
    ppermute x0 -> x51, waiting for transfers between devices: none -> 118 us  [the longest x34 73.6 us: dp_xor(): lax.ppermute(values, 'dp', [(index, index ^ bits) for index in range(size)])]
    dot_general x45 -> x0, matrix products: 118 us -> none  [the longest x10 26.2 us: matmul(): return jnp.dot(left_side, right_side, preferred_element_type=jnp.float32)]
    psum x4 -> x0, blocking collectives: 110 us -> none  [the longest x1 62.4 us: local(): lax.psum(shards[4].astype(jnp.bfloat16), 'dp').astype(jnp.float32)]
    reduce_scatter x7 -> x0, waiting for transfers between devices: 107 us -> none  [collect_rows(): lax.psum_scatter(partial_value.astype(jnp.bfloat16), 'mp', scatter_dimens...]
    convert_element_type x25 -> x19, other arithmetic: 55.4 us -> 3.38 us  [the longest x8 2.37 us: piece(): return (cut(keep) + cut(recv)).astype(jnp.bfloat16)]
    ppermute x0 -> x51, starting transfers between devices: none -> 46.9 us  [the longest x34 28.9 us: dp_xor(): lax.ppermute(values, 'dp', [(index, index ^ bits) for index in range(size)])]
  transfers between devices with their start and end apart: 16 -> 51, of which waited for: 15 -> 23; matrix products, arithmetic and copies ran while one was open for 6% -> 5% of each run, Pallas kernels for 0% -> 36%
where the time goes in v2:
time: 363 us; the launch traced here: 356 us
  Pallas kernels  151 us (42%)
  waiting for transfers between devices  118 us (33%)
  starting transfers between devices  46.9 us (13%)
  local copies, waits for them, and re-layouts  22.9 us (6%)
  other arithmetic  12.6 us (3%)
  between operations  3.98 us (1%)
    pallas_call x18, Pallas kernels, call(): pl.pallas_call(body, out_shape=shapes, in_specs=[pl.BlockSpec(memory_spac...  151 us
    ppermute x34, waiting for transfers between devices, dp_xor(): lax.ppermute(values, 'dp', [(index, index ^ bits) for index in range(size)])  73.6 us
    ppermute x8, waiting for transfers between devices, over_mp(): return lax.ppermute(values, 'mp', [(0, 1), (1, 0)])  43.4 us
    ppermute x34, starting transfers between devices, dp_xor(): lax.ppermute(values, 'dp', [(index, index ^ bits) for index in range(size)])  28.9 us
    unnamed x86, local copies, waits for them, and re-layouts  14.6 us
    ppermute x8, starting transfers between devices, over_mp(): return lax.ppermute(values, 'mp', [(0, 1), (1, 0)])  10.1 us
  transfers between devices with their start and end apart: 51, of which 23 were waited for; matrix products, arithmetic and copies ran while one was open for 5% of the time, Pallas kernels for 36%

profile of v2, /device:TPU:0, one launch (start us, length us, event | category | flops | bytes accessed | tf_op | source)
XLA Modules:
  0.0 356.0 jit_solution(10567863196209466384)
XLA Ops:
  18.2 5.2 %collective-permute-done.2.got = bf16[512,256]{1,0:T(8,128)(2,1)} collective-permute-done((bf16[512,256]{1,0:T(8,128)(2,1)}, bf16[512,256]{1,0:T(8,128)(2,1)}, u32[]{:S(2)}, u32[]{:S(2)}) %collective-permute-start.2) | collective-permute-done | bytes 262176 | tf_op jit(solution)/shard_map/ppermute | solution.py:1395
  26.6 5.3 %glu.1 = (f32[544,512]{1,0:T(8,128)}, bf16[544,512]{1,0:T(8,128)(2,1)}, bf16[544,512]{1,0:T(8,128)(2,1)}, bf16[544,512]{1,0:T(8,128)(2,1)}, bf16[544,512]{1,0:T(8,128)(2,1)}) custom-call(s32[5]{0:T(128)} %stack.119.info, bf16[512,512]{1,0:T(8,128)(2,1)} %bitcast.108, bf16[512,512]{1,0:T(8,128)(2,1)} %collective-permute-done.1.moved, ...), custom_call_target="tpu_custom_call" | custom-call | flops 10000000000 | bytes 1000000 | tf_op jit(solution)/shard_map/glu/pallas_call | solution.py:1504
  31.9 12.9 %collective-permute-done.4.got = bf16[2112,256]{1,0:T(8,128)(2,1)} collective-permute-done((bf16[2112,256]{1,0:T(8,128)(2,1)S(1)}, bf16[2112,256]{1,0:T(8,128)(2,1)}, u32[]{:S(2)}, u32[]{:S(2)}) %collective-permute-start.4) | collective-permute-done | bytes 1081376 | tf_op jit(solution)/shard_map/ppermute | solution.py:1395
  46.8 18.3 %collective-permute-done.7.got.got2 = bf16[1536,256]{1,0:T(8,128)(2,1)S(1)} collective-permute-done((bf16[1536,256]{1,0:T(8,128)(2,1)S(1)}, bf16[1536,256]{1,0:T(8,128)(2,1)S(1)}, u32[]{:S(2)}, u32[]{:S(2)}) %collective-permute-start.7) | collective-permute-done | bytes 786464 | tf_op jit(solution)/shard_map/ppermute | solution.py:1395
  66.1 15.2 %branch.1 = (f32[512,512]{1,0:T(8,128)}, bf16[8,544,256]{2,1,0:T(8,128)(2,1)}, f32[544,256]{1,0:T(8,128)}, f32[544,128]{1,0:T(8,128)}, bf16[8,512,256]{2,1,0:T(8,128)(2,1)}) custom-call(s32[5]{0:T(128)} %stack.119.info, bf16[544,512]{1,0:T(8,128)(2,1)} %get-tuple-element.157.branch, f32[544,512]{1,0:T(8,128)} %get-tuple-element.158.resid_one, ...), custom_call_target="tpu_custom_call" | custom-call | flops 10000000000 | bytes 1000000 | tf_op jit(solution)/shard_map/branch/pallas_call | solution.py:1504
  92.5 14.9 %attend.1 = (bf16[512,256]{1,0:T(8,128)(2,1)}, f32[4,512]{1,0:T(4,128)}, bf16[512,256]{1,0:T(8,128)(2,1)}, f32[4,512]{1,0:T(4,128)}) custom-call(s32[5]{0:T(128)} %stack.119.info, bf16[512,512]{1,0:T(8,128)(2,1)} %queries.1.q, bf16[512,1024]{1,0:T(8,128)(2,1)} %get-tuple-element.167.kvo, bf16[512,1024]{1,0:T(8,128)(2,1)} %copy-done.25), custom_call_target="tpu_custom_call" | custom-call | flops 10000000000 | bytes 1000000 | tf_op jit(solution)/shard_map/attend/pallas_call | solution.py:1504
  110.6 19.6 %ffn.1 = (bf16[512,512]{1,0:T(8,128)(2,1)}, f32[512,512]{1,0:T(8,128)}, bf16[512,512]{1,0:T(8,128)(2,1)}, f32[1,512]{1,0:T(1,128)}, bf16[2,2304,256]{2,1,0:T(8,128)(2,1)}, /*index=5*/bf16[2,2304,256]{2,1,0:T(8,128)(2,1)}) custom-call(s32[5]{0:T(128)} %stack.119.info, f32[512,512]{1,0:T(8,128)} %get-tuple-element.161.resid_two, ...), custom_call_target="tpu_custom_call" | custom-call | flops 10000000000 | bytes 1000000 | tf_op jit(solution)/shard_map/ffn/pallas_call | solution.py:1504
  130.4 8.9 %attend_back.2 = (bf16[512,256]{1,0:T(8,128)(2,1)}, f32[512,512]{1,0:T(8,128)}, bf16[512,512]{1,0:T(8,128)(2,1)}) custom-call(s32[5]{0:T(128)} %stack.119.info, bf16[512,512]{1,0:T(8,128)(2,1)} %queries.1.q, bf16[512,1024]{1,0:T(8,128)(2,1)} %get-tuple-element.167.kvo, bf16[512,1024]{1,0:T(8,128)(2,1)} %copy-done.25, ...), custom_call_target="tpu_custom_call" | custom-call | flops 10000000000 | bytes 1000000 | tf_op jit(solution)/shard_map/attend_back/pallas_call | solution.py:1504
  142.3 8.9 %attend_back.3 = (bf16[512,256]{1,0:T(8,128)(2,1)}, f32[512,512]{1,0:T(8,128)}, bf16[512,512]{1,0:T(8,128)(2,1)}) custom-call(s32[5]{0:T(128)} %stack.119.info, bf16[512,512]{1,0:T(8,128)(2,1)} %queries.1.q, bf16[512,1024]{1,0:T(8,128)(2,1)} %get-tuple-element.167.kvo, bf16[512,1024]{1,0:T(8,128)(2,1)} %copy-done.25, ...), custom_call_target="tpu_custom_call" | custom-call | flops 10000000000 | bytes 1000000 | tf_op jit(solution)/shard_map/attend_back/pallas_call | solution.py:1504
  152.1 5.3 %qkv_back_first.1 = (f32[512,512]{1,0:T(8,128)}, bf16[768,256]{1,0:T(8,128)(2,1)}, bf16[768,256]{1,0:T(8,128)(2,1)}) custom-call(s32[5]{0:T(128)} %stack.119.info, bf16[512,256]{1,0:T(8,128)(2,1)} %get-tuple-element.177.gq, f32[512,512]{1,0:T(8,128)} %get-tuple-element.185.gown, bf16[512,512]{1,0:T(8,128)(2,1)} %copy-done.33, ...), custom_call_target="tpu_custom_call" | custom-call | flops 10000000000 | bytes 1000000 | tf_op jit(solution)/shard_map/qkv_back_first/pallas_call | solution.py:1504
  161.7 6.8 %qkv_back_second.1 = (f32[512,512]{1,0:T(8,128)}, bf16[512,256]{1,0:T(8,128)(2,1)}, bf16[16,256]{1,0:T(8,128)(2,1)}, f32[1,512]{1,0:T(1,128)}, bf16[768,256]{1,0:T(8,128)(2,1)}, /*index=5*/bf16[768,256]{1,0:T(8,128)(2,1)}) custom-call(s32[5]{0:T(128)} %stack.119.info, bf16[512,256]{1,0:T(8,128)(2,1)} %get-tuple-element.182.gq, ...), custom_call_target="tpu_custom_call" | custom-call | flops 10000000000 | bytes 1000000 | tf_op jit(solution)/shard_map/qkv_back_second/pallas_call | solution.py:1504
  168.5 4.4 %point_back.1 = (bf16[2,1280,256]{2,1,0:T(8,128)(2,1)}, bf16[2,1280,256]{2,1,0:T(8,128)(2,1)}) custom-call(s32[5]{0:T(128)} %stack.119.info, bf16[512,256]{1,0:T(8,128)(2,1)} %get-tuple-element.189.gsep, bf16[8,512,256]{2,1,0:T(8,128)(2,1)} %get-tuple-element.190.depth, bf16[768,256]{1,0:T(8,128)(2,1)} %get-tuple-element.191.send0, ...), custom_call_target="tpu_custom_call" | custom-call | flops 10000000000 | bytes 1000000 | tf_op jit(solution)/shard_map/point_back/pallas_call | solution.py:1504
  173.6 12.2 %collective-permute-done.18 = bf16[1152,256]{1,0:T(8,128)(2,1)S(1)} collective-permute-done((bf16[1152,256]{1,0:T(8,128)(2,1)S(1)}, bf16[1152,256]{1,0:T(8,128)(2,1)S(1)}, u32[]{:S(2)}, u32[]{:S(2)}) %collective-permute-start.18) | collective-permute-done | bytes 589856 | tf_op jit(solution)/shard_map/ppermute | solution.py:1518
  187.9 15.4 %depth_back.1 = (bf16[8,544,256]{2,1,0:T(8,128)(2,1)}, bf16[8,544,256]{2,1,0:T(8,128)(2,1)}, f32[2,544,128]{2,1,0:T(8,128)}, f32[16,2048]{1,0:T(8,128)}) custom-call(s32[5]{0:T(128)} %stack.119.info, bf16[512,256]{1,0:T(8,128)(2,1)} %get-tuple-element.189.gsep, bf16[16,256]{1,0:T(8,128)(2,1)} %copy-done.38, ...), custom_call_target="tpu_custom_call" | custom-call | flops 10000000000 | bytes 1000000 | tf_op jit(solution)/shard_map/depth_back/pallas_call | solution.py:1504
  208.7 11.5 %branch_back.1 = (bf16[8,512,256]{2,1,0:T(8,128)(2,1)}, bf16[544,256]{1,0:T(8,128)(2,1)}, bf16[2,1536,256]{2,1,0:T(8,128)(2,1)}, bf16[2,1536,256]{2,1,0:T(8,128)(2,1)}) custom-call(s32[5]{0:T(128)} %stack.119.info, bf16[8,544,256]{2,1,0:T(8,128)(2,1)} %get-tuple-element.210.unit, bf16[8,544,256]{2,1,0:T(8,128)(2,1)} %get-tuple-element.211.scaled, ...), custom_call_target="tpu_custom_call" | custom-call | flops 10000000000 | bytes 1000000 | tf_op jit(solution)/shard_map/branch_back/pallas_call | solution.py:1504
  224.2 7.7 %join_back.1 = (f32[512,512]{1,0:T(8,128)}, f32[1,512]{1,0:T(1,128)}) custom-call(s32[5]{0:T(128)} %stack.119.info, bf16[8,512,256]{2,1,0:T(8,128)(2,1)} %get-tuple-element.217.gleft, bf16[544,256]{1,0:T(8,128)(2,1)} %get-tuple-element.225.gright, f32[544,512]{1,0:T(8,128)} %get-tuple-element.158.resid_one, f32[512,512]{1,0:T(8,128)} %get-tuple-element.226.grad_two, ...), custom_call_target="tpu_custom_call" | custom-call | flops 10000000000 | bytes 1000000 | tf_op jit(solution)/shard_map/join_back/pallas_call | solution.py:1504
  234.6 7.1 %glu_back.1 = (bf16[512,512]{1,0:T(8,128)(2,1)}, bf16[2,640,256]{2,1,0:T(8,128)(2,1)}, bf16[2,640,256]{2,1,0:T(8,128)(2,1)}) custom-call(s32[5]{0:T(128)} %stack.119.info, f32[512,512]{1,0:T(8,128)} %get-tuple-element.227.grad_one, f32[1,512]{1,0:T(1,128)} %get-tuple-element.231.gain_branch_row, f32[1,512]{1,0:T(1,128)} %bitcast.123, ...), custom_call_target="tpu_custom_call" | custom-call | flops 10000000000 | bytes 1000000 | tf_op jit(solution)/shard_map/glu_back/pallas_call | solution.py:1504
  249.7 4.4 %collective-permute-done.31 = bf16[768,256]{1,0:T(8,128)(2,1)S(1)} collective-permute-done((bf16[768,256]{1,0:T(8,128)(2,1)}, bf16[768,256]{1,0:T(8,128)(2,1)S(1)}, u32[]{:S(2)}, u32[]{:S(2)}) %collective-permute-start.31) | collective-permute-done | bytes 393248 | tf_op jit(solution)/shard_map/ppermute | solution.py:1395
  254.6 8.3 %collective-permute-done.32 = bf16[768,256]{1,0:T(8,128)(2,1)S(1)} collective-permute-done((bf16[768,256]{1,0:T(8,128)(2,1)S(1)}, bf16[768,256]{1,0:T(8,128)(2,1)S(1)}, u32[]{:S(2)}, u32[]{:S(2)}) %collective-permute-start.32) | collective-permute-done | bytes 393248 | tf_op jit(solution)/shard_map/ppermute | solution.py:1518
  277.8 8.0 %collective-permute-done.39 = bf16[448,256]{1,0:T(8,128)(2,1)S(1)} collective-permute-done((bf16[448,256]{1,0:T(8,128)(2,1)S(1)}, bf16[448,256]{1,0:T(8,128)(2,1)S(1)}, u32[]{:S(2)}, u32[]{:S(2)}) %collective-permute-start.39) | collective-permute-done | bytes 229408 | tf_op jit(solution)/shard_map/ppermute | solution.py:1518
  287.3 9.7 %collective-permute-done.42 = bf16[2,448,256]{2,1,0:T(8,128)(2,1)S(1)} collective-permute-done((bf16[2,448,256]{2,1,0:T(8,128)(2,1)S(1)}, bf16[2,448,256]{2,1,0:T(8,128)(2,1)S(1)}, u32[]{:S(2)}, u32[]{:S(2)}) %collective-permute-start.42) | collective-permute-done | bytes 458784 | tf_op jit(solution)/shard_map/ppermute | solution.py:1518
  302.6 4.5 %collective-permute-done.41 = bf16[192,256]{1,0:T(8,128)(2,1)S(1)} collective-permute-done((bf16[192,256]{1,0:T(8,128)(2,1)S(1)}, bf16[192,256]{1,0:T(8,128)(2,1)S(1)}, u32[]{:S(2)}, u32[]{:S(2)}) %collective-permute-start.41) | collective-permute-done | bytes 98336 | tf_op jit(solution)/shard_map/ppermute | solution.py:1518
  307.6 10.5 %collective-permute-done.45 = bf16[2,2,448,256]{3,2,1,0:T(8,128)(2,1)S(1)} collective-permute-done((bf16[2,2,448,256]{3,2,1,0:T(8,128)(2,1)S(1)}, bf16[2,2,448,256]{3,2,1,0:T(8,128)(2,1)S(1)}, u32[]{:S(2)}, u32[]{:S(2)}) %collective-permute-start.45) | collective-permute-done | bytes 917536 | tf_op jit(solution)/shard_map/ppermute | solution.py:1518
  328.4 6.0 %unpack_layout_early.1 = (f32[3,512,256]{2,1,0:T(8,128)}, f32[1024,256]{1,0:T(8,128)}, f32[512,1024]{1,0:T(8,128)}, f32[1024,512]{1,0:T(8,128)}, f32[256,512]{1,0:T(8,128)}) custom-call(s32[5]{0:T(128)} %stack.119.info, bf16[2,2,2,448,256]{4,3,2,1,0:T(8,128)(2,1)} %copy-done.2, bf16[2,2,2,448,256]{4,3,2,1,0:T(8,128)(2,1)} %collective-permute-done.48.far), custom_call_target="tpu_custom_call" | custom-call | flops 10000000000 | bytes 1000000 | tf_op jit(solution)/shard_map/unpack_layout_early/pallas_call | solution.py:1504
  (253 shorter events, 121.1 us)
Async XLA Ops:
  3.0 22.8 %collective-permute-start.1 = (bf16[512,512]{1,0:T(8,128)(2,1)}, bf16[512,512]{1,0:T(8,128)(2,1)}, u32[]{:S(2)}, u32[]{:S(2)}) collective-permute-start(bf16[512,512]{1,0:T(8,128)(2,1)} %bitcast.107), channel_id=1, source_target_pairs={{1,2},{2,1},{5,6},{6,5},{9,10},{10,9},{13,14},{14,13},{17,18},{18,... | collective-permute-start | bytes 1572872 | tf_op jit(solution)/shard_map/ppermute | solution.py:1676
  6.2 17.2 %collective-permute-start.2 = (bf16[512,256]{1,0:T(8,128)(2,1)}, bf16[512,256]{1,0:T(8,128)(2,1)}, u32[]{:S(2)}, u32[]{:S(2)}) collective-permute-start(bf16[512,256]{1,0:T(8,128)(2,1)} %broadcast_select_fusion), channel_id=1, source_target_pairs={{0,1},{1,0},{2,3},{3,2},{4,5},{5,4},{6,7},{7,6},{8,9},{9,8},{10,11... | collective-permute-start | bytes 786440 | tf_op jit(solution)/shard_map/ppermute | solution.py:1395
  18.2 26.7 %collective-permute-start.4 = (bf16[2112,256]{1,0:T(8,128)(2,1)S(1)}, bf16[2112,256]{1,0:T(8,128)(2,1)}, u32[]{:S(2)}, u32[]{:S(2)}) collective-permute-start(bf16[2112,256]{1,0:T(8,128)(2,1)S(1)} %fusion.4), channel_id=1, source_target_pairs={{0,1},{1,0},{2,3},{3,2},{4,5},{5,4},{6,7},{7,6},{8,9},{9,8},{10,11... | collective-permute-start | bytes 3244040 | tf_op jit(solution)/shard_map/ppermute | solution.py:1395
  44.8 20.3 %collective-permute-start.5 = (bf16[2112,256]{1,0:T(8,128)(2,1)}, bf16[2112,256]{1,0:T(8,128)(2,1)S(1)}, u32[]{:S(2)}, u32[]{:S(2)}) collective-permute-start(bf16[2112,256]{1,0:T(8,128)(2,1)} %collective-permute-done.4.got), channel_id=1, source_target_pairs={{0,2},{2,0},{4,6},{6,4},{8,10},{10,8},{12,14},{14,12},{16,18},{18,... | collective-permute-start | bytes 3244040 | tf_op jit(solution)/shard_map/ppermute | solution.py:1518
  45.1 20.0 %collective-permute-start.7 = (bf16[1536,256]{1,0:T(8,128)(2,1)S(1)}, bf16[1536,256]{1,0:T(8,128)(2,1)S(1)}, u32[]{:S(2)}, u32[]{:S(2)}) collective-permute-start(bf16[1536,256]{1,0:T(8,128)(2,1)S(1)} %maximum_select_fusion), channel_id=1, source_target_pairs={{0,1},{1,0},{2,3},{3,2},{4,5},{5,4},{6,7},{7,6},{8,9},{9,8},{10,11... | collective-permute-start | bytes 2359304 | tf_op jit(solution)/shard_map/ppermute | solution.py:1395
  45.9 41.4 %collective-permute-start.6 = (bf16[512,512]{1,0:T(8,128)(2,1)S(1)}, bf16[512,512]{1,0:T(8,128)(2,1)S(1)}, u32[]{:S(2)}, u32[]{:S(2)}) collective-permute-start(bf16[512,512]{1,0:T(8,128)(2,1)S(1)} %bitcast.116), channel_id=1, source_target_pairs={{1,2},{2,1},{5,6},{6,5},{9,10},{10,9},{13,14},{14,13},{17,18},{18,... | collective-permute-start | bytes 1572872 | tf_op jit(solution)/shard_map/ppermute | solution.py:1688
  65.1 16.3 %collective-permute-start.8 = (bf16[1536,256]{1,0:T(8,128)(2,1)S(1)}, bf16[1536,256]{1,0:T(8,128)(2,1)S(1)}, u32[]{:S(2)}, u32[]{:S(2)}) collective-permute-start(bf16[1536,256]{1,0:T(8,128)(2,1)S(1)} %collective-permute-done.7.got.got2), channel_id=1, source_target_pairs={{0,2},{2,0},{4,6},{6,4},{8,10},{10,8},{12,14},{14,12},{16,18},{18,... | collective-permute-start | bytes 2359304 | tf_op jit(solution)/shard_map/ppermute | solution.py:1518
  87.3 20.0 %collective-permute-start.10 = (bf16[1536,256]{1,0:T(8,128)(2,1)S(1)}, bf16[1536,256]{1,0:T(8,128)(2,1)S(1)}, u32[]{:S(2)}, u32[]{:S(2)}) collective-permute-start(bf16[1536,256]{1,0:T(8,128)(2,1)S(1)} %maximum_select_fusion.1), channel_id=1, source_target_pairs={{0,1},{1,0},{2,3},{3,2},{4,5},{5,4},{6,7},{7,6},{8,9},{9,8},{10,11... | collective-permute-start | bytes 2359304 | tf_op jit(solution)/shard_map/ppermute | solution.py:1395
  157.4 16.2 %collective-permute-start.17 = (bf16[1152,256]{1,0:T(8,128)(2,1)S(1)}, bf16[1152,256]{1,0:T(8,128)(2,1)S(1)}, u32[]{:S(2)}, u32[]{:S(2)}) collective-permute-start(bf16[1152,256]{1,0:T(8,128)(2,1)S(1)} %get-tuple-element.296), channel_id=1, source_target_pairs={{0,1},{1,0},{2,3},{3,2},{4,5},{5,4},{6,7},{7,6},{8,9},{9,8},{10,11... | collective-permute-start | bytes 1769480 | tf_op jit(solution)/shard_map/ppermute | solution.py:1395
  158.7 27.1 %collective-permute-start.18 = (bf16[1152,256]{1,0:T(8,128)(2,1)S(1)}, bf16[1152,256]{1,0:T(8,128)(2,1)S(1)}, u32[]{:S(2)}, u32[]{:S(2)}) collective-permute-start(bf16[1152,256]{1,0:T(8,128)(2,1)S(1)} %get-tuple-element.294), channel_id=1, source_target_pairs={{0,4},{2,6},{4,0},{6,2},{8,12},{10,14},{12,8},{14,10},{16,20},{18,... | collective-permute-start | bytes 1769480 | tf_op jit(solution)/shard_map/ppermute | solution.py:1518
  160.2 26.8 %collective-permute-start.19 = (bf16[1152,256]{1,0:T(8,128)(2,1)S(1)}, bf16[1152,256]{1,0:T(8,128)(2,1)S(1)}, u32[]{:S(2)}, u32[]{:S(2)}) collective-permute-start(bf16[1152,256]{1,0:T(8,128)(2,1)S(1)} %get-tuple-element.295), channel_id=1, source_target_pairs={{0,5},{1,4},{2,7},{3,6},{4,1},{5,0},{6,3},{7,2},{8,13},{9,12},{10,... | collective-permute-start | bytes 1769480 | tf_op jit(solution)/shard_map/ppermute | solution.py:1526
  172.9 30.5 %collective-permute-start.16 = (bf16[2,1280,256]{2,1,0:T(8,128)(2,1)}, bf16[2,1280,256]{2,1,0:T(8,128)(2,1)S(1)}, u32[]{:S(2)}, u32[]{:S(2)}) collective-permute-start(bf16[2,1280,256]{2,1,0:T(8,128)(2,1)} %get-tuple-element.195), channel_id=1, source_target_pairs={{0,2},{2,0},{4,6},{6,4},{8,10},{10,8},{12,14},{14,12},{16,18},{18,... | collective-permute-start | bytes 3932168 | tf_op jit(solution)/shard_map/ppermute | solution.py:1518
  204.9 15.3 %collective-permute-start.22 = (bf16[640,256]{1,0:T(8,128)(2,1)S(1)}, bf16[640,256]{1,0:T(8,128)(2,1)S(1)}, u32[]{:S(2)}, u32[]{:S(2)}) collective-permute-start(bf16[640,256]{1,0:T(8,128)(2,1)S(1)} %get-tuple-element.312), channel_id=1, source_target_pairs={{0,1},{1,0},{2,3},{3,2},{4,5},{5,4},{6,7},{7,6},{8,9},{9,8},{10,11... | collective-permute-start | bytes 983048 | tf_op jit(solution)/shard_map/ppermute | solution.py:1395
  206.2 16.1 %collective-permute-start.23 = (bf16[640,256]{1,0:T(8,128)(2,1)S(1)}, bf16[640,256]{1,0:T(8,128)(2,1)S(1)}, u32[]{:S(2)}, u32[]{:S(2)}) collective-permute-start(bf16[640,256]{1,0:T(8,128)(2,1)S(1)} %get-tuple-element.310), channel_id=1, source_target_pairs={{0,4},{2,6},{4,0},{6,2},{8,12},{10,14},{12,8},{14,10},{16,20},{18,... | collective-permute-start | bytes 983048 | tf_op jit(solution)/shard_map/ppermute | solution.py:1518
  222.5 22.9 %collective-permute-start.27 = (bf16[896,256]{1,0:T(8,128)(2,1)S(1)}, bf16[896,256]{1,0:T(8,128)(2,1)S(1)}, u32[]{:S(2)}, u32[]{:S(2)}) collective-permute-start(bf16[896,256]{1,0:T(8,128)(2,1)S(1)} %get-tuple-element.324), channel_id=1, source_target_pairs={{0,8},{2,10},{4,12},{6,14},{8,0},{10,2},{12,4},{14,6},{16,24},{18,... | collective-permute-start | bytes 1376264 | tf_op jit(solution)/shard_map/ppermute | solution.py:1518
  243.0 19.9 %collective-permute-start.32 = (bf16[768,256]{1,0:T(8,128)(2,1)S(1)}, bf16[768,256]{1,0:T(8,128)(2,1)S(1)}, u32[]{:S(2)}, u32[]{:S(2)}) collective-permute-start(bf16[768,256]{1,0:T(8,128)(2,1)S(1)} %get-tuple-element.302), channel_id=1, source_target_pairs={{0,4},{2,6},{4,0},{6,2},{8,12},{10,14},{12,8},{14,10},{16,20},{18,... | collective-permute-start | bytes 1179656 | tf_op jit(solution)/shard_map/ppermute | solution.py:1518
  243.5 19.4 %collective-permute-start.33 = (bf16[768,256]{1,0:T(8,128)(2,1)S(1)}, bf16[768,256]{1,0:T(8,128)(2,1)S(1)}, u32[]{:S(2)}, u32[]{:S(2)}) collective-permute-start(bf16[768,256]{1,0:T(8,128)(2,1)S(1)} %get-tuple-element.303), channel_id=1, source_target_pairs={{0,5},{1,4},{2,7},{3,6},{4,1},{5,0},{6,3},{7,2},{8,13},{9,12},{10,... | collective-permute-start | bytes 1179656 | tf_op jit(solution)/shard_map/ppermute | solution.py:1526
  245.6 24.5 %collective-permute-start.36 = (bf16[448,256]{1,0:T(8,128)(2,1)S(1)}, bf16[448,256]{1,0:T(8,128)(2,1)S(1)}, u32[]{:S(2)}, u32[]{:S(2)}) collective-permute-start(bf16[448,256]{1,0:T(8,128)(2,1)S(1)} %get-tuple-element.334), channel_id=1, source_target_pairs={{0,16},{2,18},{4,20},{6,22},{8,24},{10,26},{12,28},{14,30},{16,0},... | collective-permute-start | bytes 688136 | tf_op jit(solution)/shard_map/ppermute | solution.py:1518
  248.5 17.6 %collective-permute-start.28 = (bf16[320,256]{1,0:T(8,128)(2,1)S(1)}, bf16[320,256]{1,0:T(8,128)(2,1)S(1)}, u32[]{:S(2)}, u32[]{:S(2)}) collective-permute-start(bf16[320,256]{1,0:T(8,128)(2,1)S(1)} %get-tuple-element.328), channel_id=1, source_target_pairs={{0,1},{1,0},{2,3},{3,2},{4,5},{5,4},{6,7},{7,6},{8,9},{9,8},{10,11... | collective-permute-start | bytes 491528 | tf_op jit(solution)/shard_map/ppermute | solution.py:1395
  254.1 15.4 %collective-permute-start.29 = (bf16[320,256]{1,0:T(8,128)(2,1)S(1)}, bf16[320,256]{1,0:T(8,128)(2,1)S(1)}, u32[]{:S(2)}, u32[]{:S(2)}) collective-permute-start(bf16[320,256]{1,0:T(8,128)(2,1)S(1)} %get-tuple-element.326), channel_id=1, source_target_pairs={{0,4},{2,6},{4,0},{6,2},{8,12},{10,14},{12,8},{14,10},{16,20},{18,... | collective-permute-start | bytes 491528 | tf_op jit(solution)/shard_map/ppermute | solution.py:1518
  270.2 15.6 %collective-permute-start.39 = (bf16[448,256]{1,0:T(8,128)(2,1)S(1)}, bf16[448,256]{1,0:T(8,128)(2,1)S(1)}, u32[]{:S(2)}, u32[]{:S(2)}) collective-permute-start(bf16[448,256]{1,0:T(8,128)(2,1)S(1)} %add_convert_fusion.16), channel_id=1, source_target_pairs={{0,16},{2,18},{4,20},{6,22},{8,24},{10,26},{12,28},{14,30},{16,0},... | collective-permute-start | bytes 688136 | tf_op jit(solution)/shard_map/ppermute | solution.py:1518
  297.1 21.0 %collective-permute-start.45 = (bf16[2,2,448,256]{3,2,1,0:T(8,128)(2,1)S(1)}, bf16[2,2,448,256]{3,2,1,0:T(8,128)(2,1)S(1)}, u32[]{:S(2)}, u32[]{:S(2)}) collective-permute-start(bf16[2,2,448,256]{3,2,1,0:T(8,128)(2,1)S(1)} %pad_maximum_fusion.1), channel_id=1, source_target_pairs={{0,4},{2,6},{4,0},{6,2},{8,12},{10,14},{12,8},{14,10},{16,20},{18,... | collective-permute-start | bytes 2752520 | tf_op jit(solution)/shard_map/ppermute | solution.py:1518
  319.2 21.7 %collective-permute-start.12 = (bf16[512,512]{1,0:T(8,128)(2,1)S(1)}, bf16[512,512]{1,0:T(8,128)(2,1)S(1)}, u32[]{:S(2)}, u32[]{:S(2)}) collective-permute-start(bf16[512,512]{1,0:T(8,128)(2,1)S(1)} %copy-done.16), channel_id=1, source_target_pairs={{1,2},{2,1},{5,6},{6,5},{9,10},{10,9},{13,14},{14,13},{17,18},{18,... | collective-permute-start | bytes 1572872 | tf_op jit(solution)/shard_map/ppermute | solution.py:1763
  319.9 21.9 %collective-permute-start.25 = (bf16[512,512]{1,0:T(8,128)(2,1)S(1)}, bf16[512,512]{1,0:T(8,128)(2,1)S(1)}, u32[]{:S(2)}, u32[]{:S(2)}) collective-permute-start(bf16[512,512]{1,0:T(8,128)(2,1)S(1)} %copy-done.17), channel_id=1, source_target_pairs={{1,2},{2,1},{5,6},{6,5},{9,10},{10,9},{13,14},{14,13},{17,18},{18,... | collective-permute-start | bytes 1572872 | tf_op jit(solution)/shard_map/ppermute | solution.py:1869
  (67 other events, 424.5 us)
